TPU v7x, 256 devices: a whole 4x4x8 slice. The times are simulated.
256 devices in a mesh: tm: 32 (over x, y, z_hi), space: 8 (over z_lo, core).
Axes of the slice: x: 4, y: 4, z: 8 (z_hi: 2, z_lo: 4; z = z_hi * 4 + z_lo), core: 2. Of those that a mesh axis runs over, the one named last changes fastest.
Arguments:
- coarse_guess: float32 [32, 64, 32, 256], P('tm', 'space'), may hold values from 0 to 2
- initial: float32 [64, 32, 256], P('space'), may hold values from 0 to 2
- kappa: float32 [64, 32, 256], P('space'), may hold values from 0.2 to 2
- source: float32 [64, 32, 256], P('space'), may hold values from -0.5 to 1.5
Outputs:
- fine_states: float32 [128, 64, 32, 256], P('tm', 'space')
- point_change: float32 [32, 64, 32, 256], P('tm', 'space')
All inputs are finite; a program needn't handle non-finite values.
Results may differ from a plain program's by a relative error of at most 0.00002.
Values sent between devices are 32-bit elements; how exact they have to be, the bound alone decides.
A program may use at most 64 MiB of HBM per device.

v0:
```python
import jax
import jax.numpy as jnp
from jax import lax
from jax.sharding import PartitionSpec as P

STEPS_DEV = 4
SWEEPS = 3


step_length = 0.5


def extended_2(value, sides, width):
    for axis, dim in sides:
        size, length = (lax.axis_size(axis), value.shape[dim])
        up = [(i, (i + 1) % size) for i in range(size - 1)]
        down = [(j, i) for i, j in up]
        last = lax.slice_in_dim(value, length - width, length, axis=dim)
        initial = lax.slice_in_dim(value, 0, width, axis=dim)
        before = lax.ppermute(last, axis, up)
        after = lax.ppermute(initial, axis, down)
        value = jnp.concatenate([before, value, after], axis=dim)
    return value


def from_behind(value, axis, by):
    length = lax.axis_size(axis)
    pairs = [(i, i + by) for i in range(length) if 0 <= i + by < length]
    return lax.ppermute(value, axis, pairs)


def neighbours(field):
    return [
        field[2:, 1:-1, 1:-1],
        field[:-2, 1:-1, 1:-1],
        field[1:-1, 2:, 1:-1],
        field[1:-1, :-2, 1:-1],
        field[1:-1, 1:-1, 2:],
        field[1:-1, 1:-1, :-2],
    ]


def jacobi_sweep(state_ext, kappa_ext, right_part, time_step):
    padded_state = jnp.pad(state_ext, ((0, 0), (1, 1), (1, 1)))
    padded_kappa = jnp.pad(kappa_ext, ((0, 0), (1, 1), (1, 1)))
    conduct = padded_kappa * (1.0 + padded_state * padded_state)
    centre = conduct[1:-1, 1:-1, 1:-1]
    weights = jnp.zeros_like(right_part)
    inflow = jnp.zeros_like(right_part)
    for near_k, near_u in zip(neighbours(conduct), neighbours(padded_state)):
        face_value = 0.5 * (centre + near_k)
        weights = weights + face_value
        inflow = inflow + face_value * near_u
    return (right_part + time_step * inflow) / (1.0 + time_step * weights)


def per_device(coarse_guess, initial, kappa, source):
    rim_width = 1
    coefficients = extended_2(jnp.stack([kappa, source]), (("space", 1),), rim_width)
    kappa_ext = coefficients[0]
    source_ext = coefficients[1]
    local_depth = initial.shape[0]

    def propagate(state_now, time_step):
        right_part = state_now + time_step * source_ext[1 : 1 + local_depth]
        current = state_now
        for sweep_no in range(SWEEPS):
            extended = extended_2(current, (("space", 0),), 1)
            current = jacobi_sweep(extended, kappa_ext, right_part, time_step)
        return current

    coarse_step = STEPS_DEV * step_length
    tm_index = lax.axis_index("tm")
    is_first = tm_index == 0
    prior_state = from_behind(coarse_guess[0], "tm", 1)
    prior_state = jnp.where(is_first, initial, prior_state)
    relaxed = prior_state
    for repeat in range(STEPS_DEV):
        relaxed = propagate(relaxed, step_length)
    fresh_state = from_behind(relaxed, "tm", 1)
    fresh_state = jnp.where(is_first, initial, fresh_state)
    target = fresh_state
    for repeat in range(STEPS_DEV):
        target = propagate(target, step_length)
    coarse_terms = target - propagate(fresh_state, coarse_step)

    def advance_chain(number, carry):
        state_now, incoming = carry
        incoming = from_behind(state_now, "tm", 1)
        incoming = jnp.where(is_first, initial, incoming)
        return (propagate(incoming, coarse_step) + coarse_terms, incoming)

    own_state, before = lax.fori_loop(
        0, lax.axis_size("tm"), advance_chain, (jnp.zeros_like(initial), initial)
    )
    pieces = []
    current = before
    for repeat in range(STEPS_DEV - 1):
        current = propagate(current, step_length)
        pieces.append(current)
    pieces.append(own_state)
    return (jnp.stack(pieces, 0), (own_state - relaxed)[None])


def solution(mesh):
    return jax.shard_map(
        per_device,
        mesh=mesh,
        in_specs=(
            P("tm", "space", None, None),
            P("space", None, None),
            P("space", None, None),
            P("space", None, None),
        ),
        out_specs=(P("tm", "space", None, None), P("tm", "space", None, None)),
        check_vma=False,
    )
```

profile of v0, /device:TPU:5, one launch (start us, length us, event | category | flops | bytes accessed | tf_op | source)
XLA Modules:
  0.0 1798.4 jit_solution(3252870891500955549)
XLA Ops:
  264.4 1453.8 %while.15 = (s32[]{:T(128)}, f32[8,32,256]{2,1,0:T(8,128)S(1)}, f32[8,32,256]{2,1,0:T(8,128)}, pred[]{:T(512)}, f32[8,32,256]{2,1,0:T(8,128)S(1)}, /*index=5*/f3...) while((s32[]{:T(128)}, f32[8,32,256]{2,1,0:T(8,128)S(1)}, ...), condition=%wide.region_1.2_spmd.clone, body=%wide.region_0.1_spmd.clone.sunk | while | flops 12207987 | bytes 20652388 | solution.py:93
  311.2 19.0 %collective-permute-done = f32[8,32,256]{2,1,0:T(8,128)S(1)} collective-permute-done((f32[8,32,256]{2,1,0:T(8,128)S(1)}, f32[8,32,256]{2,1,0:T(8,128)S(1)}, u32[]{:S(2)}, u32[]{:S(2)}) %collective-permute-start) | collective-permute-done | bytes 262176 | tf_op jit(solution)/shard_map/while/body/eval_jaxpr/ppermute | solution.py:29
  356.6 19.0 %collective-permute-done = f32[8,32,256]{2,1,0:T(8,128)S(1)} collective-permute-done((f32[8,32,256]{2,1,0:T(8,128)S(1)}, f32[8,32,256]{2,1,0:T(8,128)S(1)}, u32[]{:S(2)}, u32[]{:S(2)}) %collective-permute-start) | collective-permute-done | bytes 262176 | tf_op jit(solution)/shard_map/while/body/eval_jaxpr/ppermute | solution.py:29
  402.0 19.0 %collective-permute-done = f32[8,32,256]{2,1,0:T(8,128)S(1)} collective-permute-done((f32[8,32,256]{2,1,0:T(8,128)S(1)}, f32[8,32,256]{2,1,0:T(8,128)S(1)}, u32[]{:S(2)}, u32[]{:S(2)}) %collective-permute-start) | collective-permute-done | bytes 262176 | tf_op jit(solution)/shard_map/while/body/eval_jaxpr/ppermute | solution.py:29
  494.1 19.0 %collective-permute-done = f32[8,32,256]{2,1,0:T(8,128)S(1)} collective-permute-done((f32[8,32,256]{2,1,0:T(8,128)S(1)}, f32[8,32,256]{2,1,0:T(8,128)S(1)}, u32[]{:S(2)}, u32[]{:S(2)}) %collective-permute-start) | collective-permute-done | bytes 262176 | tf_op jit(solution)/shard_map/while/body/eval_jaxpr/ppermute | solution.py:29
  539.5 19.0 %collective-permute-done = f32[8,32,256]{2,1,0:T(8,128)S(1)} collective-permute-done((f32[8,32,256]{2,1,0:T(8,128)S(1)}, f32[8,32,256]{2,1,0:T(8,128)S(1)}, u32[]{:S(2)}, u32[]{:S(2)}) %collective-permute-start) | collective-permute-done | bytes 262176 | tf_op jit(solution)/shard_map/while/body/eval_jaxpr/ppermute | solution.py:29
  584.9 19.0 %collective-permute-done = f32[8,32,256]{2,1,0:T(8,128)S(1)} collective-permute-done((f32[8,32,256]{2,1,0:T(8,128)S(1)}, f32[8,32,256]{2,1,0:T(8,128)S(1)}, u32[]{:S(2)}, u32[]{:S(2)}) %collective-permute-start) | collective-permute-done | bytes 262176 | tf_op jit(solution)/shard_map/while/body/eval_jaxpr/ppermute | solution.py:29
  630.3 19.0 %collective-permute-done = f32[8,32,256]{2,1,0:T(8,128)S(1)} collective-permute-done((f32[8,32,256]{2,1,0:T(8,128)S(1)}, f32[8,32,256]{2,1,0:T(8,128)S(1)}, u32[]{:S(2)}, u32[]{:S(2)}) %collective-permute-start) | collective-permute-done | bytes 262176 | tf_op jit(solution)/shard_map/while/body/eval_jaxpr/ppermute | solution.py:29
  675.7 19.0 %collective-permute-done = f32[8,32,256]{2,1,0:T(8,128)S(1)} collective-permute-done((f32[8,32,256]{2,1,0:T(8,128)S(1)}, f32[8,32,256]{2,1,0:T(8,128)S(1)}, u32[]{:S(2)}, u32[]{:S(2)}) %collective-permute-start) | collective-permute-done | bytes 262176 | tf_op jit(solution)/shard_map/while/body/eval_jaxpr/ppermute | solution.py:29
  721.1 19.0 %collective-permute-done = f32[8,32,256]{2,1,0:T(8,128)S(1)} collective-permute-done((f32[8,32,256]{2,1,0:T(8,128)S(1)}, f32[8,32,256]{2,1,0:T(8,128)S(1)}, u32[]{:S(2)}, u32[]{:S(2)}) %collective-permute-start) | collective-permute-done | bytes 262176 | tf_op jit(solution)/shard_map/while/body/eval_jaxpr/ppermute | solution.py:29
  766.6 19.0 %collective-permute-done = f32[8,32,256]{2,1,0:T(8,128)S(1)} collective-permute-done((f32[8,32,256]{2,1,0:T(8,128)S(1)}, f32[8,32,256]{2,1,0:T(8,128)S(1)}, u32[]{:S(2)}, u32[]{:S(2)}) %collective-permute-start) | collective-permute-done | bytes 262176 | tf_op jit(solution)/shard_map/while/body/eval_jaxpr/ppermute | solution.py:29
  812.0 19.0 %collective-permute-done = f32[8,32,256]{2,1,0:T(8,128)S(1)} collective-permute-done((f32[8,32,256]{2,1,0:T(8,128)S(1)}, f32[8,32,256]{2,1,0:T(8,128)S(1)}, u32[]{:S(2)}, u32[]{:S(2)}) %collective-permute-start) | collective-permute-done | bytes 262176 | tf_op jit(solution)/shard_map/while/body/eval_jaxpr/ppermute | solution.py:29
  857.4 19.0 %collective-permute-done = f32[8,32,256]{2,1,0:T(8,128)S(1)} collective-permute-done((f32[8,32,256]{2,1,0:T(8,128)S(1)}, f32[8,32,256]{2,1,0:T(8,128)S(1)}, u32[]{:S(2)}, u32[]{:S(2)}) %collective-permute-start) | collective-permute-done | bytes 262176 | tf_op jit(solution)/shard_map/while/body/eval_jaxpr/ppermute | solution.py:29
  902.8 19.0 %collective-permute-done = f32[8,32,256]{2,1,0:T(8,128)S(1)} collective-permute-done((f32[8,32,256]{2,1,0:T(8,128)S(1)}, f32[8,32,256]{2,1,0:T(8,128)S(1)}, u32[]{:S(2)}, u32[]{:S(2)}) %collective-permute-start) | collective-permute-done | bytes 262176 | tf_op jit(solution)/shard_map/while/body/eval_jaxpr/ppermute | solution.py:29
  948.2 19.0 %collective-permute-done = f32[8,32,256]{2,1,0:T(8,128)S(1)} collective-permute-done((f32[8,32,256]{2,1,0:T(8,128)S(1)}, f32[8,32,256]{2,1,0:T(8,128)S(1)}, u32[]{:S(2)}, u32[]{:S(2)}) %collective-permute-start) | collective-permute-done | bytes 262176 | tf_op jit(solution)/shard_map/while/body/eval_jaxpr/ppermute | solution.py:29
  993.6 19.0 %collective-permute-done = f32[8,32,256]{2,1,0:T(8,128)S(1)} collective-permute-done((f32[8,32,256]{2,1,0:T(8,128)S(1)}, f32[8,32,256]{2,1,0:T(8,128)S(1)}, u32[]{:S(2)}, u32[]{:S(2)}) %collective-permute-start) | collective-permute-done | bytes 262176 | tf_op jit(solution)/shard_map/while/body/eval_jaxpr/ppermute | solution.py:29
  1039.0 19.0 %collective-permute-done = f32[8,32,256]{2,1,0:T(8,128)S(1)} collective-permute-done((f32[8,32,256]{2,1,0:T(8,128)S(1)}, f32[8,32,256]{2,1,0:T(8,128)S(1)}, u32[]{:S(2)}, u32[]{:S(2)}) %collective-permute-start) | collective-permute-done | bytes 262176 | tf_op jit(solution)/shard_map/while/body/eval_jaxpr/ppermute | solution.py:29
  1084.4 19.0 %collective-permute-done = f32[8,32,256]{2,1,0:T(8,128)S(1)} collective-permute-done((f32[8,32,256]{2,1,0:T(8,128)S(1)}, f32[8,32,256]{2,1,0:T(8,128)S(1)}, u32[]{:S(2)}, u32[]{:S(2)}) %collective-permute-start) | collective-permute-done | bytes 262176 | tf_op jit(solution)/shard_map/while/body/eval_jaxpr/ppermute | solution.py:29
  1129.8 19.0 %collective-permute-done = f32[8,32,256]{2,1,0:T(8,128)S(1)} collective-permute-done((f32[8,32,256]{2,1,0:T(8,128)S(1)}, f32[8,32,256]{2,1,0:T(8,128)S(1)}, u32[]{:S(2)}, u32[]{:S(2)}) %collective-permute-start) | collective-permute-done | bytes 262176 | tf_op jit(solution)/shard_map/while/body/eval_jaxpr/ppermute | solution.py:29
  1175.2 19.0 %collective-permute-done = f32[8,32,256]{2,1,0:T(8,128)S(1)} collective-permute-done((f32[8,32,256]{2,1,0:T(8,128)S(1)}, f32[8,32,256]{2,1,0:T(8,128)S(1)}, u32[]{:S(2)}, u32[]{:S(2)}) %collective-permute-start) | collective-permute-done | bytes 262176 | tf_op jit(solution)/shard_map/while/body/eval_jaxpr/ppermute | solution.py:29
  1220.7 19.0 %collective-permute-done = f32[8,32,256]{2,1,0:T(8,128)S(1)} collective-permute-done((f32[8,32,256]{2,1,0:T(8,128)S(1)}, f32[8,32,256]{2,1,0:T(8,128)S(1)}, u32[]{:S(2)}, u32[]{:S(2)}) %collective-permute-start) | collective-permute-done | bytes 262176 | tf_op jit(solution)/shard_map/while/body/eval_jaxpr/ppermute | solution.py:29
  1266.1 19.0 %collective-permute-done = f32[8,32,256]{2,1,0:T(8,128)S(1)} collective-permute-done((f32[8,32,256]{2,1,0:T(8,128)S(1)}, f32[8,32,256]{2,1,0:T(8,128)S(1)}, u32[]{:S(2)}, u32[]{:S(2)}) %collective-permute-start) | collective-permute-done | bytes 262176 | tf_op jit(solution)/shard_map/while/body/eval_jaxpr/ppermute | solution.py:29
  1311.5 19.0 %collective-permute-done = f32[8,32,256]{2,1,0:T(8,128)S(1)} collective-permute-done((f32[8,32,256]{2,1,0:T(8,128)S(1)}, f32[8,32,256]{2,1,0:T(8,128)S(1)}, u32[]{:S(2)}, u32[]{:S(2)}) %collective-permute-start) | collective-permute-done | bytes 262176 | tf_op jit(solution)/shard_map/while/body/eval_jaxpr/ppermute | solution.py:29
  1356.9 19.0 %collective-permute-done = f32[8,32,256]{2,1,0:T(8,128)S(1)} collective-permute-done((f32[8,32,256]{2,1,0:T(8,128)S(1)}, f32[8,32,256]{2,1,0:T(8,128)S(1)}, u32[]{:S(2)}, u32[]{:S(2)}) %collective-permute-start) | collective-permute-done | bytes 262176 | tf_op jit(solution)/shard_map/while/body/eval_jaxpr/ppermute | solution.py:29
  (1119 shorter events, 1352.4 us)
Async XLA Ops:
  0.6 22.7 %collective-permute-start.9 = (f32[8,32,256]{2,1,0:T(8,128)}, f32[8,32,256]{2,1,0:T(8,128)S(1)}, u32[]{:S(2)}, u32[]{:S(2)}) collective-permute-start(f32[8,32,256]{2,1,0:T(8,128)} %bitcast.21), channel_id=1, source_target_pairs={{0,8},{8,16},{16,24},{24,32},{32,40},{40,48},{48,56},{56,64},{64,7... | collective-permute-start | bytes 786440 | tf_op jit(solution)/shard_map/ppermute | solution.py:29
  309.3 21.0 %collective-permute-start = (f32[8,32,256]{2,1,0:T(8,128)S(1)}, f32[8,32,256]{2,1,0:T(8,128)S(1)}, u32[]{:S(2)}, u32[]{:S(2)}) collective-permute-start(f32[8,32,256]{2,1,0:T(8,128)S(1)} %broadcast_select_fusion.6), channel_id=1, source_target_pairs={{0,8},{8,16},{16,24},{24,32},{32,40},{40,48},{48,56},{56,64},{64,7... | collective-permute-start | bytes 786440 | tf_op jit(solution)/shard_map/while/body/eval_jaxpr/ppermute | solution.py:29
  354.7 21.0 %collective-permute-start = (f32[8,32,256]{2,1,0:T(8,128)S(1)}, f32[8,32,256]{2,1,0:T(8,128)S(1)}, u32[]{:S(2)}, u32[]{:S(2)}) collective-permute-start(f32[8,32,256]{2,1,0:T(8,128)S(1)} %broadcast_select_fusion.6), channel_id=1, source_target_pairs={{0,8},{8,16},{16,24},{24,32},{32,40},{40,48},{48,56},{56,64},{64,7... | collective-permute-start | bytes 786440 | tf_op jit(solution)/shard_map/while/body/eval_jaxpr/ppermute | solution.py:29
  400.1 20.9 %collective-permute-start = (f32[8,32,256]{2,1,0:T(8,128)S(1)}, f32[8,32,256]{2,1,0:T(8,128)S(1)}, u32[]{:S(2)}, u32[]{:S(2)}) collective-permute-start(f32[8,32,256]{2,1,0:T(8,128)S(1)} %broadcast_select_fusion.6), channel_id=1, source_target_pairs={{0,8},{8,16},{16,24},{24,32},{32,40},{40,48},{48,56},{56,64},{64,7... | collective-permute-start | bytes 786440 | tf_op jit(solution)/shard_map/while/body/eval_jaxpr/ppermute | solution.py:29
  492.2 20.9 %collective-permute-start = (f32[8,32,256]{2,1,0:T(8,128)S(1)}, f32[8,32,256]{2,1,0:T(8,128)S(1)}, u32[]{:S(2)}, u32[]{:S(2)}) collective-permute-start(f32[8,32,256]{2,1,0:T(8,128)S(1)} %broadcast_select_fusion.6), channel_id=1, source_target_pairs={{0,8},{8,16},{16,24},{24,32},{32,40},{40,48},{48,56},{56,64},{64,7... | collective-permute-start | bytes 786440 | tf_op jit(solution)/shard_map/while/body/eval_jaxpr/ppermute | solution.py:29
  537.6 20.9 %collective-permute-start = (f32[8,32,256]{2,1,0:T(8,128)S(1)}, f32[8,32,256]{2,1,0:T(8,128)S(1)}, u32[]{:S(2)}, u32[]{:S(2)}) collective-permute-start(f32[8,32,256]{2,1,0:T(8,128)S(1)} %broadcast_select_fusion.6), channel_id=1, source_target_pairs={{0,8},{8,16},{16,24},{24,32},{32,40},{40,48},{48,56},{56,64},{64,7... | collective-permute-start | bytes 786440 | tf_op jit(solution)/shard_map/while/body/eval_jaxpr/ppermute | solution.py:29
  583.0 20.9 %collective-permute-start = (f32[8,32,256]{2,1,0:T(8,128)S(1)}, f32[8,32,256]{2,1,0:T(8,128)S(1)}, u32[]{:S(2)}, u32[]{:S(2)}) collective-permute-start(f32[8,32,256]{2,1,0:T(8,128)S(1)} %broadcast_select_fusion.6), channel_id=1, source_target_pairs={{0,8},{8,16},{16,24},{24,32},{32,40},{40,48},{48,56},{56,64},{64,7... | collective-permute-start | bytes 786440 | tf_op jit(solution)/shard_map/while/body/eval_jaxpr/ppermute | solution.py:29
  628.4 20.9 %collective-permute-start = (f32[8,32,256]{2,1,0:T(8,128)S(1)}, f32[8,32,256]{2,1,0:T(8,128)S(1)}, u32[]{:S(2)}, u32[]{:S(2)}) collective-permute-start(f32[8,32,256]{2,1,0:T(8,128)S(1)} %broadcast_select_fusion.6), channel_id=1, source_target_pairs={{0,8},{8,16},{16,24},{24,32},{32,40},{40,48},{48,56},{56,64},{64,7... | collective-permute-start | bytes 786440 | tf_op jit(solution)/shard_map/while/body/eval_jaxpr/ppermute | solution.py:29
  673.8 20.9 %collective-permute-start = (f32[8,32,256]{2,1,0:T(8,128)S(1)}, f32[8,32,256]{2,1,0:T(8,128)S(1)}, u32[]{:S(2)}, u32[]{:S(2)}) collective-permute-start(f32[8,32,256]{2,1,0:T(8,128)S(1)} %broadcast_select_fusion.6), channel_id=1, source_target_pairs={{0,8},{8,16},{16,24},{24,32},{32,40},{40,48},{48,56},{56,64},{64,7... | collective-permute-start | bytes 786440 | tf_op jit(solution)/shard_map/while/body/eval_jaxpr/ppermute | solution.py:29
  719.2 20.9 %collective-permute-start = (f32[8,32,256]{2,1,0:T(8,128)S(1)}, f32[8,32,256]{2,1,0:T(8,128)S(1)}, u32[]{:S(2)}, u32[]{:S(2)}) collective-permute-start(f32[8,32,256]{2,1,0:T(8,128)S(1)} %broadcast_select_fusion.6), channel_id=1, source_target_pairs={{0,8},{8,16},{16,24},{24,32},{32,40},{40,48},{48,56},{56,64},{64,7... | collective-permute-start | bytes 786440 | tf_op jit(solution)/shard_map/while/body/eval_jaxpr/ppermute | solution.py:29
  764.6 20.9 %collective-permute-start = (f32[8,32,256]{2,1,0:T(8,128)S(1)}, f32[8,32,256]{2,1,0:T(8,128)S(1)}, u32[]{:S(2)}, u32[]{:S(2)}) collective-permute-start(f32[8,32,256]{2,1,0:T(8,128)S(1)} %broadcast_select_fusion.6), channel_id=1, source_target_pairs={{0,8},{8,16},{16,24},{24,32},{32,40},{40,48},{48,56},{56,64},{64,7... | collective-permute-start | bytes 786440 | tf_op jit(solution)/shard_map/while/body/eval_jaxpr/ppermute | solution.py:29
  810.0 20.9 %collective-permute-start = (f32[8,32,256]{2,1,0:T(8,128)S(1)}, f32[8,32,256]{2,1,0:T(8,128)S(1)}, u32[]{:S(2)}, u32[]{:S(2)}) collective-permute-start(f32[8,32,256]{2,1,0:T(8,128)S(1)} %broadcast_select_fusion.6), channel_id=1, source_target_pairs={{0,8},{8,16},{16,24},{24,32},{32,40},{40,48},{48,56},{56,64},{64,7... | collective-permute-start | bytes 786440 | tf_op jit(solution)/shard_map/while/body/eval_jaxpr/ppermute | solution.py:29
  855.4 20.9 %collective-permute-start = (f32[8,32,256]{2,1,0:T(8,128)S(1)}, f32[8,32,256]{2,1,0:T(8,128)S(1)}, u32[]{:S(2)}, u32[]{:S(2)}) collective-permute-start(f32[8,32,256]{2,1,0:T(8,128)S(1)} %broadcast_select_fusion.6), channel_id=1, source_target_pairs={{0,8},{8,16},{16,24},{24,32},{32,40},{40,48},{48,56},{56,64},{64,7... | collective-permute-start | bytes 786440 | tf_op jit(solution)/shard_map/while/body/eval_jaxpr/ppermute | solution.py:29
  900.9 20.9 %collective-permute-start = (f32[8,32,256]{2,1,0:T(8,128)S(1)}, f32[8,32,256]{2,1,0:T(8,128)S(1)}, u32[]{:S(2)}, u32[]{:S(2)}) collective-permute-start(f32[8,32,256]{2,1,0:T(8,128)S(1)} %broadcast_select_fusion.6), channel_id=1, source_target_pairs={{0,8},{8,16},{16,24},{24,32},{32,40},{40,48},{48,56},{56,64},{64,7... | collective-permute-start | bytes 786440 | tf_op jit(solution)/shard_map/while/body/eval_jaxpr/ppermute | solution.py:29
  946.3 20.9 %collective-permute-start = (f32[8,32,256]{2,1,0:T(8,128)S(1)}, f32[8,32,256]{2,1,0:T(8,128)S(1)}, u32[]{:S(2)}, u32[]{:S(2)}) collective-permute-start(f32[8,32,256]{2,1,0:T(8,128)S(1)} %broadcast_select_fusion.6), channel_id=1, source_target_pairs={{0,8},{8,16},{16,24},{24,32},{32,40},{40,48},{48,56},{56,64},{64,7... | collective-permute-start | bytes 786440 | tf_op jit(solution)/shard_map/while/body/eval_jaxpr/ppermute | solution.py:29
  991.7 20.9 %collective-permute-start = (f32[8,32,256]{2,1,0:T(8,128)S(1)}, f32[8,32,256]{2,1,0:T(8,128)S(1)}, u32[]{:S(2)}, u32[]{:S(2)}) collective-permute-start(f32[8,32,256]{2,1,0:T(8,128)S(1)} %broadcast_select_fusion.6), channel_id=1, source_target_pairs={{0,8},{8,16},{16,24},{24,32},{32,40},{40,48},{48,56},{56,64},{64,7... | collective-permute-start | bytes 786440 | tf_op jit(solution)/shard_map/while/body/eval_jaxpr/ppermute | solution.py:29
  1037.1 20.9 %collective-permute-start = (f32[8,32,256]{2,1,0:T(8,128)S(1)}, f32[8,32,256]{2,1,0:T(8,128)S(1)}, u32[]{:S(2)}, u32[]{:S(2)}) collective-permute-start(f32[8,32,256]{2,1,0:T(8,128)S(1)} %broadcast_select_fusion.6), channel_id=1, source_target_pairs={{0,8},{8,16},{16,24},{24,32},{32,40},{40,48},{48,56},{56,64},{64,7... | collective-permute-start | bytes 786440 | tf_op jit(solution)/shard_map/while/body/eval_jaxpr/ppermute | solution.py:29
  1082.5 20.9 %collective-permute-start = (f32[8,32,256]{2,1,0:T(8,128)S(1)}, f32[8,32,256]{2,1,0:T(8,128)S(1)}, u32[]{:S(2)}, u32[]{:S(2)}) collective-permute-start(f32[8,32,256]{2,1,0:T(8,128)S(1)} %broadcast_select_fusion.6), channel_id=1, source_target_pairs={{0,8},{8,16},{16,24},{24,32},{32,40},{40,48},{48,56},{56,64},{64,7... | collective-permute-start | bytes 786440 | tf_op jit(solution)/shard_map/while/body/eval_jaxpr/ppermute | solution.py:29
  1127.9 20.9 %collective-permute-start = (f32[8,32,256]{2,1,0:T(8,128)S(1)}, f32[8,32,256]{2,1,0:T(8,128)S(1)}, u32[]{:S(2)}, u32[]{:S(2)}) collective-permute-start(f32[8,32,256]{2,1,0:T(8,128)S(1)} %broadcast_select_fusion.6), channel_id=1, source_target_pairs={{0,8},{8,16},{16,24},{24,32},{32,40},{40,48},{48,56},{56,64},{64,7... | collective-permute-start | bytes 786440 | tf_op jit(solution)/shard_map/while/body/eval_jaxpr/ppermute | solution.py:29
  1173.3 20.9 %collective-permute-start = (f32[8,32,256]{2,1,0:T(8,128)S(1)}, f32[8,32,256]{2,1,0:T(8,128)S(1)}, u32[]{:S(2)}, u32[]{:S(2)}) collective-permute-start(f32[8,32,256]{2,1,0:T(8,128)S(1)} %broadcast_select_fusion.6), channel_id=1, source_target_pairs={{0,8},{8,16},{16,24},{24,32},{32,40},{40,48},{48,56},{56,64},{64,7... | collective-permute-start | bytes 786440 | tf_op jit(solution)/shard_map/while/body/eval_jaxpr/ppermute | solution.py:29
  1218.7 20.9 %collective-permute-start = (f32[8,32,256]{2,1,0:T(8,128)S(1)}, f32[8,32,256]{2,1,0:T(8,128)S(1)}, u32[]{:S(2)}, u32[]{:S(2)}) collective-permute-start(f32[8,32,256]{2,1,0:T(8,128)S(1)} %broadcast_select_fusion.6), channel_id=1, source_target_pairs={{0,8},{8,16},{16,24},{24,32},{32,40},{40,48},{48,56},{56,64},{64,7... | collective-permute-start | bytes 786440 | tf_op jit(solution)/shard_map/while/body/eval_jaxpr/ppermute | solution.py:29
  1264.1 20.9 %collective-permute-start = (f32[8,32,256]{2,1,0:T(8,128)S(1)}, f32[8,32,256]{2,1,0:T(8,128)S(1)}, u32[]{:S(2)}, u32[]{:S(2)}) collective-permute-start(f32[8,32,256]{2,1,0:T(8,128)S(1)} %broadcast_select_fusion.6), channel_id=1, source_target_pairs={{0,8},{8,16},{16,24},{24,32},{32,40},{40,48},{48,56},{56,64},{64,7... | collective-permute-start | bytes 786440 | tf_op jit(solution)/shard_map/while/body/eval_jaxpr/ppermute | solution.py:29
  1309.5 20.9 %collective-permute-start = (f32[8,32,256]{2,1,0:T(8,128)S(1)}, f32[8,32,256]{2,1,0:T(8,128)S(1)}, u32[]{:S(2)}, u32[]{:S(2)}) collective-permute-start(f32[8,32,256]{2,1,0:T(8,128)S(1)} %broadcast_select_fusion.6), channel_id=1, source_target_pairs={{0,8},{8,16},{16,24},{24,32},{32,40},{40,48},{48,56},{56,64},{64,7... | collective-permute-start | bytes 786440 | tf_op jit(solution)/shard_map/while/body/eval_jaxpr/ppermute | solution.py:29
  1355.0 20.9 %collective-permute-start = (f32[8,32,256]{2,1,0:T(8,128)S(1)}, f32[8,32,256]{2,1,0:T(8,128)S(1)}, u32[]{:S(2)}, u32[]{:S(2)}) collective-permute-start(f32[8,32,256]{2,1,0:T(8,128)S(1)} %broadcast_select_fusion.6), channel_id=1, source_target_pairs={{0,8},{8,16},{16,24},{24,32},{32,40},{40,48},{48,56},{56,64},{64,7... | collective-permute-start | bytes 786440 | tf_op jit(solution)/shard_map/while/body/eval_jaxpr/ppermute | solution.py:29
  (315 other events, 2495.9 us)
where the time goes:
time: 1820 us; the launch traced here: 1800 us
  waiting for transfers between devices  818 us (45%)
  starting transfers between devices  814 us (45%)
  other arithmetic  154 us (8%)
    ppermute x34, waiting for transfers between devices, from_behind(): return lax.ppermute(value, axis, pairs)  621 us
    ppermute x132, starting transfers between devices, extended_2(): before = lax.ppermute(last, axis, up)  471 us
    ppermute x132, starting transfers between devices, extended_2(): after = lax.ppermute(initial, axis, down)  269 us
    ppermute x132, waiting for transfers between devices, extended_2(): before = lax.ppermute(last, axis, up)  101 us
    ppermute x132, waiting for transfers between devices, extended_2(): after = lax.ppermute(initial, axis, down)  95.8 us
    ppermute x34, starting transfers between devices, from_behind(): return lax.ppermute(value, axis, pairs)  74.2 us
    div x96, other arithmetic, jacobi_sweep(): return (right_part + time_step * inflow) / (1.0 + time_step * weights)  68.2 us
    mul x130, other arithmetic, jacobi_sweep(): conduct = padded_kappa * (1.0 + padded_state * padded_state)  54.6 us
  transfers between devices with their start and end apart: 298, of which 164 were waited for; matrix products, arithmetic and copies ran while one was open for 0% of the time, Pallas kernels for 0%

commit v1 on v0

v1 whole, which is shorter than its diff:
```python
import functools

import jax
import jax.numpy as jnp
from jax import lax
from jax.experimental import pallas as pl
from jax.experimental.pallas import tpu as pltpu
from jax.sharding import PartitionSpec as P

MESH = pl.DeviceIdType.MESH
STEPS_DEV = 4
SWEEPS = 3
FINE_STEP = 0.5
COARSE_STEP = STEPS_DEV * FINE_STEP
H = SWEEPS
WINDOW = 6


def kernel(
    n_tm, n_sp, cg, u0, kap, src, fine, pc,
    V, F, KP, HS, T1, T2, K, G, NAT, CT, CTB, REL, OWN,
    cs_sem, cr_sem, hs_sem, hr_sem, fs_sem, fr_sem,
    rel_s, rel_r, bef_s, bef_r, own_s, own_r, ct_s, ct_r, credit,
):
    depth, nx, ny = u0.shape
    xf_n = nx // 8
    half = ny // 2
    top = depth + 2 * H
    t, s = lax.axis_index("tm"), lax.axis_index("space")
    home = n_tm - 1
    is_home = t == home
    has_lo, has_hi = s > 0, s < n_sp - 1
    sides = ((0, has_lo, s - 1), (1, has_hi, s + 1))
    t_next, t_prev = lax.rem(t + 1, n_tm), lax.rem(t + n_tm - 1, n_tm)
    inner = pl.ds(H, depth)

    barrier = pltpu.get_barrier_semaphore()

    def greet(tt, ss):
        pl.semaphore_signal(barrier, inc=1, device_id=(tt, ss), device_id_type=MESH)

    for _, there, ss in sides:
        @pl.when(there)
        def _():
            greet(t, ss)
    greet(t_next, s)
    greet(t_prev, s)

    @pl.when(is_home)
    def _():
        def one(i, c):
            greet(i, s)
            return c
        lax.fori_loop(0, home, one, 0)

    @pl.when(jnp.logical_not(is_home))
    def _():
        greet(home, s)

    row = lax.broadcasted_iota(jnp.int32, (ny, ny), 0)
    col = lax.broadcasted_iota(jnp.int32, (ny, ny), 1)
    want = jnp.where(col < half, 2 * col, 2 * (col - half) + 1)
    split_y = jnp.where(row == want, 1.0, 0.0)
    want_t = jnp.where(row < half, 2 * row, 2 * (row - half) + 1)
    join_y = jnp.where(col == want_t, 1.0, 0.0)

    def permute(rows, matrix):
        return jnp.dot(rows, matrix, precision=lax.Precision.HIGHEST, preferred_element_type=jnp.float32)

    def to_inside(value, put):
        moved = permute(value.reshape(depth * nx, ny), split_y)
        for h in range(2):
            NAT[h] = moved[:, h * half : (h + 1) * half].reshape(depth, nx, half)
        for z in range(depth):
            for xf in range(xf_n):
                for h in range(2):
                    put(z, xf, h, NAT[h, z, pl.ds(xf, 8, stride=xf_n), :])

    def to_outside(get, out):
        for z in range(depth):
            for xf in range(xf_n):
                for h in range(2):
                    NAT[h, z, pl.ds(xf, 8, stride=xf_n), :] = get(z, xf, h)
        rows = jnp.concatenate([NAT[0].reshape(depth * nx, half), NAT[1].reshape(depth * nx, half)], axis=1)
        out[...] = permute(rows, join_y).reshape(depth, nx, ny)

    def lanes(h):
        return slice(h * half, (h + 1) * half)

    def put_start(z, xf, h, x):
        V[0, H + z, xf, :, lanes(h)] = x

    def put_first(z, xf, h, x):
        F[0, H + z, xf, :, lanes(h)] = x

    def put_kap(z, xf, h, x):
        KP[0, H + z, xf, :, lanes(h)] = (0.5 * FINE_STEP) * x

    def put_src(z, xf, h, x):
        HS[0, H + z, xf, :, lanes(h)] = FINE_STEP * x

    to_inside(jnp.where(is_home, u0[...], cg[0]), put_start)
    to_inside(kap[...], put_kap)
    to_inside(src[...], put_src)

    def blank(lo):
        zero = jnp.zeros((H,) + KP.shape[2:], jnp.float32)
        KP[0, pl.ds(lo, H)] = zero
        HS[0, pl.ds(lo, H)] = zero

        def one(i, c):
            V[i, pl.ds(lo, H)] = zero
            return c
        lax.fori_loop(0, V.shape[0], one, 0)

        def two(i, c):
            F[i, pl.ds(lo, H)] = zero
            return c
        lax.fori_loop(0, F.shape[0], two, 0)

    @pl.when(jnp.logical_not(has_lo))
    def _():
        blank(0)

    @pl.when(jnp.logical_not(has_hi))
    def _():
        blank(H + depth)

    greeted = has_lo.astype(jnp.int32) + has_hi.astype(jnp.int32) + 2 + jnp.where(is_home, home, 1)
    pl.semaphore_wait(barrier, greeted)

    def edge(buf, side):
        own = buf.at[pl.ds(H, H)] if side == 0 else buf.at[pl.ds(depth, H)]
        far = buf.at[pl.ds(H + depth, H)] if side == 0 else buf.at[pl.ds(0, H)]
        near = buf.at[pl.ds(0, H)] if side == 0 else buf.at[pl.ds(H + depth, H)]
        return own, far, near

    def halo(buf, send, recv, start):
        for side, there, ss in sides:
            own, far, near = edge(buf, side)

            @pl.when(there)
            def _():
                if start:
                    pltpu.make_async_remote_copy(
                        src_ref=own, dst_ref=far, send_sem=send.at[side], recv_sem=recv.at[1 - side],
                        device_id=(t, ss), device_id_type=MESH).start()
                else:
                    copy = pltpu.make_async_remote_copy(
                        src_ref=own, dst_ref=near, send_sem=send.at[side], recv_sem=recv.at[side],
                        device_id=(t, ss), device_id_type=MESH)
                    copy.wait_send()
                    copy.wait_recv()

    halo(V.at[0], hs_sem.at[0], hr_sem.at[0], True)
    halo(KP.at[0], cs_sem.at[0], cr_sem.at[0], True)
    halo(HS.at[0], cs_sem.at[1], cr_sem.at[1], True)

    lane = lax.broadcasted_iota(jnp.int32, (8, half), 1)
    sub = lax.broadcasted_iota(jnp.int32, (8, half), 0)
    l_first, l_last, s_first, s_last = lane == 0, lane == half - 1, sub == 0, sub == 7
    mask_lo = jnp.where(has_lo, 1.0, 0.0)
    mask_hi = jnp.where(has_hi, 1.0, 0.0)

    def conduct(U, coef, which, z):
        for xf in range(xf_n):
            v, kp = U[z, xf], KP[coef, z, xf]
            k = kp + kp * (v * v)
            K[which, z, xf] = k
            G[which, z, xf] = k * v

    def around(A, z):
        c = [[A[z, xf, :, lanes(h)] for h in range(2)] for xf in range(xf_n)]
        sums = []
        for xf in range(xf_n):
            even, odd = c[xf]
            left = jnp.where(l_first, 0.0, pltpu.roll(odd, 1, 1))
            right = jnp.where(l_last, 0.0, pltpu.roll(even, half - 1, 1))
            along = (left + odd, even + right)
            both = []
            for h in range(2):
                up = c[xf - 1][h] if xf > 0 else jnp.where(s_first, 0.0, pltpu.roll(c[-1][h], 1, 0))
                down = c[xf + 1][h] if xf < xf_n - 1 else jnp.where(s_last, 0.0, pltpu.roll(c[0][h], 7, 0))
                both.append((A[z - 1, xf, :, lanes(h)] + A[z + 1, xf, :, lanes(h)]) + (up + down) + along[h])
            sums.append(both)
        return c, sums

    def relax(U, U0, coef, which, z, out, masked):
        kc, ks = around(K.at[which], z)
        _, vs = around(U, z)
        _, gs = around(G.at[which], z)
        if masked:
            keep = jnp.where(z < H, mask_lo, jnp.where(z >= H + depth, mask_hi, 1.0))
        for xf in range(xf_n):
            for h in range(2):
                k = kc[xf][h]
                right_part = U0[z, xf, :, lanes(h)] + HS[coef, z, xf, :, lanes(h)]
                num = (right_part + gs[xf][h]) + k * vs[xf][h]
                den = (1.0 + ks[xf][h]) + 6.0 * k
                r = pltpu.reciprocal(den, approx=True)
                r = r * (2.0 - den * r)
                value = num * r
                out[z, xf, :, lanes(h)] = value * keep if masked else value

    def span(body, starts, count, unroll):
        def one(i, c):
            for z in starts:
                body(z + i)
            return c
        lax.fori_loop(0, count, one, 0, unroll=unroll)

    last = H + depth

    def early(U, coef, out):
        span(lambda z: conduct(U, coef, 0, z), (H, H + depth // 2), depth // 2, 2)
        span(lambda z: relax(U, U, coef, 0, z, T1, False), (H + 1, H + depth // 2), depth // 2 - 1, 1)
        span(lambda z: conduct(T1, coef, 1, z), (H + 1, H + depth // 2), depth // 2 - 1, 3)
        span(lambda z: relax(T1, U, coef, 1, z, T2, False), (H + 2, H + depth // 2), depth // 2 - 2, 1)
        span(lambda z: conduct(T2, coef, 2, z), (H + 2, H + depth // 2), depth // 2 - 2, 2)
        span(lambda z: relax(T2, U, coef, 2, z, out, False), (H + 3, H + depth // 2), depth // 2 - 3, 1)

    def late(U, coef, out):
        span(lambda z: conduct(U, coef, 0, z), (0, last), H, H)
        span(lambda z: relax(U, U, coef, 0, z, T1, True), (1, last - 1), H, 1)
        span(lambda z: conduct(T1, coef, 1, z), (1, last - 1), H, H)
        span(lambda z: relax(T1, U, coef, 1, z, T2, True), (2, last - 2), H, 1)
        span(lambda z: conduct(T2, coef, 2, z), (2, last - 2), H, H)
        span(lambda z: relax(T2, U, coef, 2, z, out, False), (3, last - 3), H, 1)

    def each(body):
        def one(z, c):
            for xf in range(xf_n):
                body(z, xf)
            return c
        lax.fori_loop(0, depth, one, 0, unroll=2)

    early(V.at[0], 0, V.at[1])
    halo(KP.at[0], cs_sem.at[0], cr_sem.at[0], False)
    halo(HS.at[0], cs_sem.at[1], cr_sem.at[1], False)
    halo(V.at[0], hs_sem.at[0], hr_sem.at[0], False)

    def scale(z, c):
        for xf in range(xf_n):
            KP[1, z, xf] = STEPS_DEV * KP[0, z, xf]
            HS[1, z, xf] = STEPS_DEV * HS[0, z, xf]
        return c
    lax.fori_loop(0, top, scale, 0, unroll=2)
    late(V.at[0], 0, V.at[1])

    def step(n, c):
        par = lax.rem(n, 2)
        halo(V.at[n], hs_sem.at[par], hr_sem.at[par], True)

        @pl.when(n == STEPS_DEV + 1)
        def _():
            U = V.at[STEPS_DEV]
            early(U, 1, F.at[1])
            late(U, 1, F.at[1])

            def keep(z, xf):
                CT[z, xf] = F[1, H + z, xf]
            each(keep)
        early(V.at[n], 0, V.at[n + 1])
        halo(V.at[n], hs_sem.at[par], hr_sem.at[par], False)
        late(V.at[n], 0, V.at[n + 1])
        return c
    lax.fori_loop(1, 2 * STEPS_DEV, step, 0)

    def rel_copy():
        return pltpu.make_async_remote_copy(
            src_ref=V.at[STEPS_DEV, inner], dst_ref=REL, send_sem=rel_s, recv_sem=rel_r,
            device_id=(t_next, s), device_id_type=MESH)

    def ct_copy(i):
        return pltpu.make_async_remote_copy(
            src_ref=CT, dst_ref=CTB.at[i], send_sem=ct_s, recv_sem=ct_r.at[i],
            device_id=(home, s), device_id_type=MESH)

    def bef_copy(n, i):
        return pltpu.make_async_remote_copy(
            src_ref=V.at[n, inner], dst_ref=F.at[0, inner], send_sem=bef_s.at[i], recv_sem=bef_r,
            device_id=(i, s), device_id_type=MESH)

    def own_copy():
        return pltpu.make_async_remote_copy(
            src_ref=F.at[0, inner], dst_ref=OWN, send_sem=own_s, recv_sem=own_r,
            device_id=(t_prev, s), device_id_type=MESH)

    n_terms = n_tm - 2
    first = 2 * STEPS_DEV

    @pl.when(is_home)
    def _():
        rel_copy().start()
        bef_copy(STEPS_DEV, 1).start()

        def advance(i, c):
            n = first + i
            par = lax.rem(n, 2)
            halo(V.at[n], hs_sem.at[par], hr_sem.at[par], True)
            bef_copy(n, i + 2).start()
            early(V.at[n], 1, V.at[n + 1])
            halo(V.at[n], hs_sem.at[par], hr_sem.at[par], False)
            late(V.at[n], 1, V.at[n + 1])
            ct_copy(i).wait_recv()

            def add(z, xf):
                V[n + 1, H + z, xf] = V[n + 1, H + z, xf] + CTB[i, z, xf]
            each(add)

            @pl.when(i + WINDOW < n_terms)
            def _():
                pl.semaphore_signal(credit, inc=1, device_id=(i + WINDOW, s), device_id_type=MESH)
            return c
        lax.fori_loop(0, n_terms - 1, advance, 0)

        def take(z, xf):
            F[0, H + z, xf] = V[first + n_terms - 1, H + z, xf]
        each(take)

    @pl.when(jnp.logical_not(is_home))
    def _():
        @pl.when(t < n_terms)
        def _():
            def term(z, xf):
                CT[z, xf] = V[2 * STEPS_DEV, H + z, xf] - CT[z, xf]
            each(term)

            @pl.when(t >= WINDOW)
            def _():
                pl.semaphore_wait(credit, 1)
            ct_copy(t).start()

        @pl.when(t == n_terms)
        def _():
            rel_copy().start()

        @pl.when(t == 0)
        def _():
            to_inside(u0[...], put_first)

        @pl.when(t > 0)
        def _():
            bef_copy(0, t).wait_recv()

        @pl.when(t != n_terms)
        def _():
            rel_copy().start()

    @pl.when(t > 0)
    def _():
        own_copy().start()

    for i in range(STEPS_DEV - 1):
        par = i % 2
        halo(F.at[i], fs_sem.at[par], fr_sem.at[par], True)
        if i == 1:
            @pl.when(is_home)
            def _():
                early(F.at[0], 1, V.at[0])
                late(F.at[0], 1, V.at[0])
                ct_copy(n_terms - 1).wait_recv()

                def total(z, xf):
                    OWN[z, xf] = V[0, H + z, xf] + CTB[n_terms - 1, z, xf]
                each(total)
        early(F.at[i], 0, F.at[i + 1])
        halo(F.at[i], fs_sem.at[par], fr_sem.at[par], False)
        late(F.at[i], 0, F.at[i + 1])

    for i in range(STEPS_DEV - 1):
        to_outside(lambda z, xf, h: F[i + 1, H + z, xf, :, lanes(h)], fine.at[i])

    @pl.when(jnp.logical_not(is_home))
    def _():
        own_copy().wait_recv()
    rel_copy().wait_recv()
    to_outside(lambda z, xf, h: OWN[z, xf, :, lanes(h)], fine.at[STEPS_DEV - 1])
    to_outside(lambda z, xf, h: OWN[z, xf, :, lanes(h)] - REL[z, xf, :, lanes(h)], pc.at[0])

    rel_copy().wait_send()

    @pl.when(t > 0)
    def _():
        own_copy().wait_send()

    @pl.when(t < n_terms)
    def _():
        ct_copy(t).wait_send()

    @pl.when(is_home)
    def _():
        def one(i, c):
            bef_copy(0, i).wait_send()
            return c
        lax.fori_loop(1, home, one, 0)


def solution(mesh):
    n_tm, n_sp = mesh.shape["tm"], mesh.shape["space"]

    def per_device(coarse_guess, initial, kappa, source):
        depth, nx, ny = initial.shape
        plane = (nx // 8, 8, ny)
        top = depth + 2 * H
        n_terms = n_tm - 2
        dma = pltpu.SemaphoreType.DMA
        whole = pl.BlockSpec(memory_space=pltpu.VMEM)
        f32 = jnp.float32
        return pl.pallas_call(
            functools.partial(kernel, n_tm, n_sp),
            out_shape=(
                jax.ShapeDtypeStruct((STEPS_DEV, depth, nx, ny), f32),
                jax.ShapeDtypeStruct((1, depth, nx, ny), f32),
            ),
            in_specs=[whole] * 4,
            out_specs=(whole, whole),
            scratch_shapes=[
                pltpu.VMEM((2 * STEPS_DEV + n_terms, top) + plane, f32),
                pltpu.VMEM((STEPS_DEV, top) + plane, f32),
                pltpu.VMEM((2, top) + plane, f32),
                pltpu.VMEM((2, top) + plane, f32),
                pltpu.VMEM((top,) + plane, f32),
                pltpu.VMEM((top,) + plane, f32),
                pltpu.VMEM((SWEEPS, top) + plane, f32),
                pltpu.VMEM((SWEEPS, top) + plane, f32),
                pltpu.VMEM((2, depth, nx, ny // 2), f32),
                pltpu.VMEM((depth,) + plane, f32),
                pltpu.VMEM((n_terms, depth) + plane, f32),
                pltpu.VMEM((depth,) + plane, f32),
                pltpu.VMEM((depth,) + plane, f32),
                dma((2, 2)), dma((2, 2)), dma((2, 2)), dma((2, 2)), dma((2, 2)), dma((2, 2)),
                dma, dma, dma((n_tm,)), dma, dma, dma, dma, dma((n_tm,)),
                pltpu.SemaphoreType.REGULAR,
            ],
            compiler_params=pltpu.CompilerParams(
                collective_id=0, has_side_effects=True, vmem_limit_bytes=56 * 1024 * 1024
            ),
        )(coarse_guess, initial, kappa, source)

    return jax.shard_map(
        per_device,
        mesh=mesh,
        in_specs=(
            P("tm", "space", None, None),
            P("space", None, None),
            P("space", None, None),
            P("space", None, None),
        ),
        out_specs=(P("tm", "space", None, None), P("tm", "space", None, None)),
        check_vma=False,
    )
```

time: 1820 us -> 315 us (0.17)
  the two profiles are of different devices: /device:TPU:5 before, /device:TPU:31 now
where the time goes in v1:
time: 315 us
  Pallas kernels  311 us (99%)
    pallas_call x1, Pallas kernels, per_device(): pl.pallas_call(functools.partial(kernel, n_tm, n_sp), out_shape=(jax.Shap...  311 us

profile of v1, /device:TPU:31, one launch (start us, length us, event | category | flops | bytes accessed | tf_op | source)
XLA Modules:
  0.0 315.0 jit_solution(16347424986422304195)
XLA Ops:
  0.6 311.3 %shard_map.59 = (f32[4,8,32,256]{3,2,1,0:T(8,128)}, f32[1,8,32,256]{3,2,1,0:T(8,128)}) custom-call(f32[1,8,32,256]{3,2,1,0:T(8,128)} %cg.1, f32[8,32,256]{2,1,0:T(8,128)} %u0.1, f32[8,32,256]{2,1,0:T(8,128)} %kap.1, f32[8,32,256]{2,1,0:T(8,128)} %src.1), custom_call_target="tpu_custom_call" | custom-call | tf_op jit(solution)/shard_map/pallas_call | solution.py:410
  311.9 0.0 copy-start
  311.9 2.4 copy.8
  314.3 0.0 copy-done
  314.3 0.7 copy.9
Async XLA Ops:
  311.9 2.4 copy-start

commit v2 on v0

v2 whole, which is shorter than its diff:
```python
import functools

import jax
import jax.numpy as jnp
from jax import lax
from jax.experimental import pallas as pl
from jax.experimental.pallas import tpu as pltpu
from jax.sharding import PartitionSpec as P

MESH = pl.DeviceIdType.MESH
STEPS_DEV = 4
SWEEPS = 3
FINE_STEP = 0.5
COARSE_STEP = STEPS_DEV * FINE_STEP
FAR = 2 * SWEEPS
NEAR = SWEEPS
WINDOW = 8


def kernel(
    n_tm, n_sp, cg, u0, kap, src, fine, pc,
    V, F, KP, HS, T, K, G, NAT, CT, CTB, REL, OWN,
    cf_s, cf_r, vf_s, vf_r, vn_s, vn_r, ff_s, ff_r, fn_s, fn_r,
    rel_s, rel_r, bef_s, bef_r, own_r, ct_s, ct_r, credit,
):
    depth, nx, ny = u0.shape
    xf_n = nx // 8
    half = ny // 2
    top = FAR + depth + NEAR
    t, s = lax.axis_index("tm"), lax.axis_index("space")
    n_slab = n_tm - 2
    zh = lax.rem(t, 2)
    is_home = t >= n_slab
    not_home = t < n_slab
    odd = lax.rem(s, 2)
    near_s = s + 1 - 2 * odd
    far_s = s - 1 + 2 * odd
    has_far = (far_s >= 0) & (far_s < n_sp)
    far_i = has_far.astype(jnp.int32)
    t_next, t_prev = lax.rem(t + 1, n_tm), lax.rem(t + n_tm - 1, n_tm)
    base, sign = odd * (top - 1), 1 - 2 * odd

    def at(p):
        return base + sign * p

    def lowest(p, count):
        return at(p) - odd * (count - 1)

    def layers(p, count):
        return pl.ds(lowest(p, count), count)

    own_lo = lowest(FAR, depth)
    inner = pl.ds(own_lo, depth)

    barrier = pltpu.get_barrier_semaphore()

    def greet(tt, ss):
        pl.semaphore_signal(barrier, inc=1, device_id=(tt, ss), device_id_type=MESH)

    greet(t, near_s)
    greet(t_next, s)
    greet(t_prev, s)

    @pl.when(has_far)
    def _():
        greet(t, far_s)

    @pl.when(is_home)
    def _():
        def one(i, c):
            greet(i, s)

            @pl.when(has_far)
            def _():
                greet(i, far_s)
            return c
        lax.fori_loop(0, n_slab, one, 0)

    @pl.when(not_home)
    def _():
        for h in range(2):
            greet(n_slab + h, s)

            @pl.when(has_far)
            def _():
                greet(n_slab + h, far_s)

    row = lax.broadcasted_iota(jnp.int32, (ny, ny), 0)
    col = lax.broadcasted_iota(jnp.int32, (ny, ny), 1)
    want = jnp.where(col < half, 2 * col, 2 * (col - half) + 1)
    split_y = jnp.where(row == want, 1.0, 0.0)
    want_t = jnp.where(row < half, 2 * row, 2 * (row - half) + 1)
    join_y = jnp.where(col == want_t, 1.0, 0.0)

    def permute(rows, matrix):
        return jnp.dot(rows, matrix, precision=lax.Precision.HIGHEST, preferred_element_type=jnp.float32)

    def lanes(h):
        return slice(h * half, (h + 1) * half)

    def to_inside(value, dst, scale):
        moved = permute(value.reshape(depth * nx, ny), split_y)
        for h in range(2):
            NAT[h] = moved[:, h * half : (h + 1) * half].reshape(depth, nx, half)

        def one(z, c):
            dst[own_lo + z] = jnp.stack([
                jnp.concatenate([scale * NAT[h, z, pl.ds(xf, 8, stride=xf_n), :] for h in range(2)], axis=1)
                for xf in range(xf_n)], axis=0)
            return c
        lax.fori_loop(0, depth, one, 0)

    def to_outside(get, out):
        def one(z, c):
            layer = get(z)
            for xf in range(xf_n):
                for h in range(2):
                    NAT[h, z, pl.ds(xf, 8, stride=xf_n), :] = layer[xf, :, lanes(h)]
            return c
        lax.fori_loop(0, depth, one, 0)
        rows = jnp.concatenate([NAT[0].reshape(depth * nx, half), NAT[1].reshape(depth * nx, half)], axis=1)
        out[...] = permute(rows, join_y).reshape(depth, nx, ny)

    to_inside(jnp.where(is_home, u0[...], cg[0]), V.at[0], 1.0)

    @pl.when(t == n_slab)
    def _():
        to_inside(cg[0], V.at[2 * STEPS_DEV + n_slab + 2], 1.0)
    to_inside(kap[...], KP.at[0], 0.5 * FINE_STEP)
    to_inside(src[...], HS.at[0], FINE_STEP)

    @pl.when(jnp.logical_not(has_far))
    def _():
        zero = jnp.zeros((FAR,) + KP.shape[2:], jnp.float32)
        KP[0, layers(0, FAR)] = zero
        HS[0, layers(0, FAR)] = zero

        def one(i, c):
            V[2 * i, layers(0, FAR)] = zero
            return c
        lax.fori_loop(0, V.shape[0] // 2, one, 0)

        def two(i, c):
            CTB[i, pl.ds(lowest(NEAR, NEAR) - NEAR, NEAR)] = zero[:NEAR]
            return c
        lax.fori_loop(0, n_slab, two, 0)
        for i in (0, 2):
            F[i, layers(0, FAR)] = zero

    greeted = 3 + far_i + jnp.where(is_home, n_slab, 2) * (1 + far_i)
    pl.semaphore_wait(barrier, greeted)

    def remote(src_ref, dst_ref, send, recv, tt, ss):
        return pltpu.make_async_remote_copy(
            src_ref=src_ref, dst_ref=dst_ref, send_sem=send, recv_sem=recv, device_id=(tt, ss), device_id_type=MESH)

    def far_copy(buf, send, recv, j):
        there = (1 - odd) * (top - 1) + (2 * odd - 1) * (FAR - 1 - j)
        return remote(buf.at[at(FAR + j)], buf.at[there], send.at[j], recv.at[j], t, far_s)

    def near_copy(buf, send, recv):
        own = lowest(FAR + depth - NEAR, NEAR)
        there = odd * (top - NEAR)
        return remote(buf.at[pl.ds(own, NEAR)], buf.at[pl.ds(there, NEAR)], send, recv, t, near_s)

    def far_start(buf, send, recv):
        @pl.when(has_far)
        def _():
            for j in range(FAR):
                far_copy(buf, send, recv, j).start()

    def far_wait(buf, send, recv, js):
        @pl.when(has_far)
        def _():
            for j in js:
                copy = far_copy(buf, send, recv, j)
                copy.wait_send()
                copy.wait_recv()

    def near_wait(buf, send, recv):
        copy = near_copy(buf, send, recv)
        copy.wait_send()
        copy.wait_recv()

    near_copy(V.at[0], vn_s.at[0], vn_r.at[0]).start()
    near_copy(KP.at[0], cf_s.at[0, FAR], cf_r.at[0, FAR]).start()
    near_copy(HS.at[0], cf_s.at[1, FAR], cf_r.at[1, FAR]).start()
    far_start(V.at[0], vf_s.at[0], vf_r.at[0])
    far_start(KP.at[0], cf_s.at[0], cf_r.at[0])
    far_start(HS.at[0], cf_s.at[1], cf_r.at[1])

    lane = lax.broadcasted_iota(jnp.int32, (8, half), 1)
    sub = lax.broadcasted_iota(jnp.int32, (8, half), 0)
    l_first, l_last, s_first, s_last = lane == 0, lane == half - 1, sub == 0, sub == 7
    mask_far = jnp.where(has_far, 1.0, 0.0)

    def conduct(U, coef, which, p):
        z = at(p)
        v, kp = U[z], KP[coef, z]
        k = kp + kp * (v * v)
        K[which, z] = k
        G[which, z] = k * v

    def around(A, z):
        here, both_z = A[z], A[z - 1] + A[z + 1]
        c = [[here[xf, :, lanes(h)] for h in range(2)] for xf in range(xf_n)]
        sums = []
        for xf in range(xf_n):
            even_y, odd_y = c[xf]
            left = jnp.where(l_first, 0.0, pltpu.roll(odd_y, 1, 1))
            right = jnp.where(l_last, 0.0, pltpu.roll(even_y, half - 1, 1))
            along = (left + odd_y, even_y + right)
            both = []
            for h in range(2):
                up = c[xf - 1][h] if xf > 0 else jnp.where(s_first, 0.0, pltpu.roll(c[-1][h], 1, 0))
                down = c[xf + 1][h] if xf < xf_n - 1 else jnp.where(s_last, 0.0, pltpu.roll(c[0][h], 7, 0))
                both.append(both_z[xf, :, lanes(h)] + (up + down) + along[h])
            sums.append(both)
        return c, sums

    def relax(U, U0, coef, which, p, out, term, masked):
        z = at(p)
        kc, ks = around(K.at[which], z)
        _, vs = around(U, z)
        _, gs = around(G.at[which], z)
        if masked:
            keep = jnp.where(p < FAR, mask_far, 1.0)
        right_part = U0[z] + HS[coef, z]
        if term is not None:
            extra_term = term[z - NEAR]
        rows = []
        for xf in range(xf_n):
            parts = []
            for h in range(2):
                k = kc[xf][h]
                num = (right_part[xf, :, lanes(h)] + gs[xf][h]) + k * vs[xf][h]
                den = (1.0 + ks[xf][h]) + 6.0 * k
                r = pltpu.reciprocal(den, approx=True)
                r = r * (2.0 - den * r)
                value = num * r
                if masked:
                    value = value * keep
                if term is not None:
                    value = value + extra_term[xf, :, lanes(h)]
                parts.append(value)
            rows.append(jnp.concatenate(parts, axis=1))
        out[z] = jnp.stack(rows, axis=0)

    def span(body, p, count, width):
        turns = count // width
        if turns == 1:
            for k in range(width):
                body(p + k)
        else:
            def one(i, c):
                for k in range(width):
                    body(p + i * width + k)
                return c
            lax.fori_loop(0, turns, one, 0)
        for k in range(turns * width, count):
            body(p + k)

    first, end = FAR, FAR + depth

    def pair(states, n, coefs, terms, waits, far, near):
        U0, U1, U2 = states(n), states(n + 1), states(n + 2)
        far_send, far_recv = far
        near_send, near_recv = near
        c0, c1 = coefs
        term0, term1 = terms
        steps = (
            (U0, c0, (T.at[0], T.at[1], U1), term0),
            (U1, c1, (T.at[2], T.at[3], U2), term1),
        )

        def cond(i, k, p):
            U, c, outs, _ = steps[i]
            conduct(U if k == 0 else outs[k - 1], c, 3 * i + k, p)

        def sweep(i, k, p, masked):
            U, c, outs, term = steps[i]
            relax(U if k == 0 else outs[k - 1], U, c, 3 * i + k, p, outs[k], term if k == 2 else None, masked)

        for i in range(2):
            lo = first + SWEEPS * i
            span(lambda p: cond(i, 0, p), lo, end - lo, 4 if i == 0 else 5)
            span(lambda p: sweep(i, 0, p, False), lo + 1, end - lo - 2, 3)
            near_wait(steps[i][0], near_send.at[i], near_recv.at[i])
            span(lambda p: cond(i, 0, p), end, NEAR, NEAR)
            span(lambda p: sweep(i, 0, p, False), end - 1, NEAR, NEAR)
            span(lambda p: cond(i, 1, p), lo + 1, end + 1 - lo, 3)
            span(lambda p: sweep(i, 1, p, False), lo + 2, end - 1 - lo, 4)
            span(lambda p: cond(i, 2, p), lo + 2, end - 1 - lo, 4)
            waits(i)
            span(lambda p: sweep(i, 2, p, False), lo + 3, end - 3 - lo, 5 if i == 0 else 2)
            if i == 0:
                near_copy(U1, near_send.at[1], near_recv.at[1]).start()

        def wave(j, c):
            @pl.when(has_far)
            def _():
                for k in range(2):
                    copy = far_copy(U0, far_send, far_recv, 2 * j + k)
                    copy.wait_send()
                    copy.wait_recv()
            p = first - 1 - 2 * j
            for i in range(2):
                for k in range(SWEEPS):
                    cond(i, k, p)
                    cond(i, k, p - 1)
                    p = p + 1
                    sweep(i, k, p, True)
                    sweep(i, k, p - 1, True)
            return c
        lax.fori_loop(0, FAR // 2, wave, 0)

    def v_state(n):
        return V.at[n]

    def f_state(n):
        return F.at[n]

    def no_wait(i):
        pass

    def each(body):
        def one(z, c):
            body(z)
            return c
        lax.fori_loop(0, depth, one, 0)

    near_wait(KP.at[0], cf_s.at[0, FAR], cf_r.at[0, FAR])
    near_wait(HS.at[0], cf_s.at[1, FAR], cf_r.at[1, FAR])
    far_wait(KP.at[0], cf_s.at[0], cf_r.at[0], range(FAR))
    far_wait(HS.at[0], cf_s.at[1], cf_r.at[1], range(FAR))

    def scale(z, c):
        KP[1, z] = STEPS_DEV * KP[0, z]
        HS[1, z] = STEPS_DEV * HS[0, z]
        return c
    lax.fori_loop(0, top, scale, 0)

    def v_pair(n, coefs, terms, waits):
        par = lax.rem(lax.div(n, 2), 2)
        pair(v_state, n, coefs, terms, waits, (vf_s.at[par], vf_r.at[par]), (vn_s, vn_r))

    def v_send(n):
        par = lax.rem(lax.div(n, 2), 2)
        near_copy(V.at[n], vn_s.at[0], vn_r.at[0]).start()
        far_start(V.at[n], vf_s.at[par], vf_r.at[par])

    extra = 2 * STEPS_DEV + n_slab + 2

    def fine_pair(m, c):
        n = 2 * m + lax.div(m, STEPS_DEV) * (extra - 2 * STEPS_DEV)

        @pl.when(m > 0)
        def _():
            v_send(n)
        v_pair(n, (0, 0), (None, None), no_wait)

        @pl.when(m == STEPS_DEV // 2)
        def _():
            U = V.at[STEPS_DEV]
            span(lambda p: conduct(U, 1, 0, p), NEAR, top - NEAR, 4)
            span(lambda p: relax(U, U, 1, 0, p, T.at[0], None, True), NEAR + 1, top - NEAR - 2, 4)
            span(lambda p: conduct(T.at[0], 1, 1, p), NEAR + 1, top - NEAR - 2, 4)
            span(lambda p: relax(T.at[0], U, 1, 1, p, T.at[1], None, True), NEAR + 2, top - NEAR - 4, 4)
            span(lambda p: conduct(T.at[1], 1, 2, p), NEAR + 2, top - NEAR - 4, 4)
            span(lambda p: relax(T.at[1], U, 1, 2, p, T.at[2], None, False), first, depth, 4)

            def keep(z):
                CT[z] = T[2, own_lo + z]
            each(keep)
        return c
    lax.fori_loop(0, STEPS_DEV + lax.div(t, n_slab) * (1 - zh) * (STEPS_DEV // 2), fine_pair, 0)

    def rel_copy(n, tt, k):
        return remote(V.at[n, inner], REL, rel_s.at[k], rel_r, tt, s)

    def ct_copy(i, h):
        return remote(CT, CTB.at[i, pl.ds(own_lo - NEAR, depth)], ct_s.at[h, 0], ct_r.at[i, 0], n_slab + h, s)

    def ct_far_copy(i, h):
        mine = odd * (depth - NEAR)
        there = (1 - odd) * depth
        return remote(CT.at[pl.ds(mine, NEAR)], CTB.at[i, pl.ds(there, NEAR)], ct_s.at[h, 1], ct_r.at[i, 1], n_slab + h, far_s)

    def bef_copy(n, i):
        return remote(V.at[n, inner], F.at[0, inner], bef_s.at[i, 0], bef_r, i, s)

    def own_copy(n, i):
        return remote(V.at[n, inner], OWN, bef_s.at[i, 1], own_r, i, s)

    begin = 2 * STEPS_DEV - 1

    def hand_out(d, n):
        to_own = lax.rem(d + zh, 2) == 0

        @pl.when(to_own & (d < n_slab))
        def _():
            own_copy(n, d).start()

        @pl.when(jnp.logical_not(to_own) & (d + 1 < n_slab))
        def _():
            bef_copy(n, d + 1).start()

    def f_pair(n, par):
        near_copy(F.at[n], fn_s.at[0], fn_r.at[0]).start()
        far_start(F.at[n], ff_s.at[par], ff_r.at[par])
        pair(f_state, n, (0, 0), (None, None), no_wait, (ff_s.at[par], ff_r.at[par]), (fn_s, fn_r))

    def f_both(c):
        def one(m, c):
            f_pair(2 * m, m)
            return c
        lax.fori_loop(0, 2, one, 0)

    def take(n):
        def one(z):
            F[0, own_lo + z] = V[n, own_lo + z]
        each(one)

    @pl.when(is_home)
    def _():
        hand_out(0, STEPS_DEV)

        @pl.when(zh == 0)
        def _():
            rel_copy(STEPS_DEV, 0, 0).start()
            rel_copy(extra + STEPS_DEV, t_next, 1).start()

    @pl.when(t == 0)
    def _():
        to_inside(u0[...], F.at[0], 1.0)

    @pl.when(is_home)
    def _():
        def advance(i, c):
            n = 2 * STEPS_DEV + 2 * i
            v_send(n)
            hand_out(2 * i + 1, n)

            def waits(k):
                ct_copy(2 * i + k, 0).wait_recv()
                if k == 0:
                    @pl.when(has_far)
                    def _():
                        ct_far_copy(2 * i, 0).wait_recv()
            v_pair(n, (1, 1), (CTB.at[2 * i], CTB.at[2 * i + 1]), waits)
            hand_out(2 * i + 2, n + 1)
            for k in range(2):
                @pl.when(2 * i + k + WINDOW < n_slab)
                def _():
                    pl.semaphore_signal(
                        credit.at[zh], inc=1, device_id=(2 * i + k + WINDOW, s), device_id_type=MESH)
            return c
        lax.fori_loop(0, n_slab // 2, advance, 0)

        def last(z):
            OWN[z] = V[begin + n_slab + zh, own_lo + z]
        each(last)

    @pl.when(not_home)
    def _():
        def term(z):
            CT[z] = V[2 * STEPS_DEV, own_lo + z] - CT[z]
        each(term)
        for h in range(2):
            @pl.when(t >= WINDOW)
            def _():
                pl.semaphore_wait(credit.at[h], 1)
            ct_copy(t, h).start()

            @pl.when((zh == 0) & has_far)
            def _():
                ct_far_copy(t, h).start()

        @pl.when(t > 0)
        def _():
            bef_copy(0, t).wait_recv()
        rel_copy(STEPS_DEV, t_next, 0).start()

    @pl.when(is_home)
    def _():
        take(begin + n_slab - 1 + zh)
    f_both(0)

    for i in range(STEPS_DEV - 1):
        to_outside(lambda z: F[i + 1, own_lo + z], fine.at[i])

    @pl.when(not_home)
    def _():
        own_copy(0, t).wait_recv()
    rel_copy(STEPS_DEV, t_next, 0).wait_recv()
    to_outside(lambda z: OWN[z], fine.at[STEPS_DEV - 1])
    to_outside(lambda z: OWN[z] - REL[z], pc.at[0])

    @pl.when(not_home)
    def _():
        rel_copy(STEPS_DEV, t_next, 0).wait_send()
        for h in range(2):
            ct_copy(t, h).wait_send()

            @pl.when((zh == 0) & has_far)
            def _():
                ct_far_copy(t, h).wait_send()

    @pl.when(t == n_slab)
    def _():
        for k in range(2):
            rel_copy(STEPS_DEV, 0, k).wait_send()

    @pl.when(is_home)
    def _():
        def one(i, c):
            @pl.when(lax.rem(i + zh, 2) == 0)
            def _():
                own_copy(0, i).wait_send()

                @pl.when(i > 0)
                def _():
                    bef_copy(0, i).wait_send()
            return c
        lax.fori_loop(0, n_slab, one, 0)


def solution(mesh):
    n_tm, n_sp = mesh.shape["tm"], mesh.shape["space"]

    def per_device(coarse_guess, initial, kappa, source):
        depth, nx, ny = initial.shape
        plane = (nx // 8, 8, ny)
        top = FAR + depth + NEAR
        n_terms = n_tm - 2
        dma = pltpu.SemaphoreType.DMA
        whole = pl.BlockSpec(memory_space=pltpu.VMEM)
        f32 = jnp.float32
        return pl.pallas_call(
            functools.partial(kernel, n_tm, n_sp),
            out_shape=(
                jax.ShapeDtypeStruct((STEPS_DEV, depth, nx, ny), f32),
                jax.ShapeDtypeStruct((1, depth, nx, ny), f32),
            ),
            in_specs=[whole] * 4,
            out_specs=(whole, whole),
            scratch_shapes=[
                pltpu.VMEM((3 * STEPS_DEV + 3 + n_terms, top) + plane, f32),
                pltpu.VMEM((STEPS_DEV + 1, top) + plane, f32),
                pltpu.VMEM((2, top) + plane, f32),
                pltpu.VMEM((2, top) + plane, f32),
                pltpu.VMEM((4, top) + plane, f32),
                pltpu.VMEM((2 * SWEEPS, top) + plane, f32),
                pltpu.VMEM((2 * SWEEPS, top) + plane, f32),
                pltpu.VMEM((2, depth, nx, ny // 2), f32),
                pltpu.VMEM((depth,) + plane, f32),
                pltpu.VMEM((n_terms, depth + NEAR) + plane, f32),
                pltpu.VMEM((depth,) + plane, f32),
                pltpu.VMEM((depth,) + plane, f32),
                dma((2, FAR + 1)), dma((2, FAR + 1)),
                dma((2, FAR)), dma((2, FAR)), dma((2,)), dma((2,)),
                dma((2, FAR)), dma((2, FAR)), dma((2,)), dma((2,)),
                dma((2,)), dma, dma((n_tm, 2)), dma, dma, dma((2, 2)), dma((n_tm, 2)),
                pltpu.SemaphoreType.REGULAR((2,)),
            ],
            compiler_params=pltpu.CompilerParams(
                collective_id=0, has_side_effects=True, vmem_limit_bytes=56 * 1024 * 1024
            ),
        )(coarse_guess, initial, kappa, source)

    return jax.shard_map(
        per_device,
        mesh=mesh,
        in_specs=(
            P("tm", "space", None, None),
            P("space", None, None),
            P("space", None, None),
            P("space", None, None),
        ),
        out_specs=(P("tm", "space", None, None), P("tm", "space", None, None)),
        check_vma=False,
    )
```

time: 1820 us -> 227 us (0.12)
  the two profiles are of different devices: /device:TPU:5 before, /device:TPU:151 now
where the time goes in v2:
time: 227 us; the launch traced here: 223 us
  Pallas kernels  220 us (97%)
  local copies, waits for them, and re-layouts  3.06 us (1%)
    pallas_call x1, Pallas kernels, per_device(): pl.pallas_call(functools.partial(kernel, n_tm, n_sp), out_shape=(jax.Shap...  220 us

profile of v2, /device:TPU:151, one launch (start us, length us, event | category | flops | bytes accessed | tf_op | source)
XLA Modules:
  0.0 223.2 jit_solution(15434782350949296767)
XLA Ops:
  0.6 219.5 %shard_map.59 = (f32[4,8,32,256]{3,2,1,0:T(8,128)}, f32[1,8,32,256]{3,2,1,0:T(8,128)}) custom-call(f32[1,8,32,256]{3,2,1,0:T(8,128)} %cg.1, f32[8,32,256]{2,1,0:T(8,128)} %u0.1, f32[8,32,256]{2,1,0:T(8,128)} %kap.1, f32[8,32,256]{2,1,0:T(8,128)} %src.1), custom_call_target="tpu_custom_call" | custom-call | tf_op jit(solution)/shard_map/pallas_call | solution.py:539
  220.2 0.0 copy-start
  220.2 2.4 %copy.8 = f32[4,8,32,256]{3,2,1,0:T(8,128)} copy(f32[4,8,32,256]{3,2,1,0:T(8,128)} %get-tuple-element.4) | data formatting | bytes 2097152
  222.5 0.0 copy-done
  222.5 0.7 copy.9
Async XLA Ops:
  220.2 2.4 %copy-start = (f32[1,8,32,256]{3,2,1,0:T(8,128)S(1)}, f32[1,8,32,256]{3,2,1,0:T(8,128)}, u32[]{:S(2)}) copy-start(f32[1,8,32,256]{3,2,1,0:T(8,128)} %get-tuple-element.5) | copy-start | bytes 786436

commit v3 on v2

--- a/solution.py
+++ b/solution.py
@@ -21,7 +21,7 @@
     n_tm, n_sp, cg, u0, kap, src, fine, pc,
     V, F, KP, HS, T, K, G, NAT, CT, CTB, REL, OWN,
     cf_s, cf_r, vf_s, vf_r, vn_s, vn_r, ff_s, ff_r, fn_s, fn_r,
-    rel_s, rel_r, bef_s, bef_r, own_r, ct_s, ct_r, credit,
+    rel_s, rel_r, bef_s, bef_r, own_r, ct_s, ct_r, th_s, th_r, credit,
 ):
     depth, nx, ny = u0.shape
     xf_n = nx // 8
@@ -69,10 +69,6 @@
     def _():
         def one(i, c):
             greet(i, s)
-
-            @pl.when(has_far)
-            def _():
-                greet(i, far_s)
             return c
         lax.fori_loop(0, n_slab, one, 0)
 
@@ -80,10 +76,6 @@
     def _():
         for h in range(2):
             greet(n_slab + h, s)
-
-            @pl.when(has_far)
-            def _():
-                greet(n_slab + h, far_s)
 
     row = lax.broadcasted_iota(jnp.int32, (ny, ny), 0)
     col = lax.broadcasted_iota(jnp.int32, (ny, ny), 1)
@@ -147,7 +139,7 @@
         for i in (0, 2):
             F[i, layers(0, FAR)] = zero
 
-    greeted = 3 + far_i + jnp.where(is_home, n_slab, 2) * (1 + far_i)
+    greeted = 3 + far_i + jnp.where(is_home, n_slab, 2)
     pl.semaphore_wait(barrier, greeted)
 
     def remote(src_ref, dst_ref, send, recv, tt, ss):
@@ -155,8 +147,8 @@
             src_ref=src_ref, dst_ref=dst_ref, send_sem=send, recv_sem=recv, device_id=(tt, ss), device_id_type=MESH)
 
     def far_copy(buf, send, recv, j):
-        there = (1 - odd) * (top - 1) + (2 * odd - 1) * (FAR - 1 - j)
-        return remote(buf.at[at(FAR + j)], buf.at[there], send.at[j], recv.at[j], t, far_s)
+        there = (1 - odd) * (top - FAR + 2 * j) + odd * (FAR - 2 - 2 * j)
+        return remote(buf.at[layers(FAR + 2 * j, 2)], buf.at[pl.ds(there, 2)], send.at[j], recv.at[j], t, far_s)
 
     def near_copy(buf, send, recv):
         own = lowest(FAR + depth - NEAR, NEAR)
@@ -166,7 +158,7 @@
     def far_start(buf, send, recv):
         @pl.when(has_far)
         def _():
-            for j in range(FAR):
+            for j in range(FAR // 2):
                 far_copy(buf, send, recv, j).start()
 
     def far_wait(buf, send, recv, js):
@@ -235,9 +227,7 @@
                 k = kc[xf][h]
                 num = (right_part[xf, :, lanes(h)] + gs[xf][h]) + k * vs[xf][h]
                 den = (1.0 + ks[xf][h]) + 6.0 * k
-                r = pltpu.reciprocal(den, approx=True)
-                r = r * (2.0 - den * r)
-                value = num * r
+                value = num * pltpu.reciprocal(den, approx=True)
                 if masked:
                     value = value * keep
                 if term is not None:
@@ -262,7 +252,7 @@
 
     first, end = FAR, FAR + depth
 
-    def pair(states, n, coefs, terms, waits, far, near):
+    def pair(states, n, coefs, terms, waits, far, near, hook, second):
         U0, U1, U2 = states(n), states(n + 1), states(n + 2)
         far_send, far_recv = far
         near_send, near_recv = near
@@ -281,7 +271,7 @@
             U, c, outs, term = steps[i]
             relax(U if k == 0 else outs[k - 1], U, c, 3 * i + k, p, outs[k], term if k == 2 else None, masked)
 
-        for i in range(2):
+        def early(i):
             lo = first + SWEEPS * i
             span(lambda p: cond(i, 0, p), lo, end - lo, 4 if i == 0 else 5)
             span(lambda p: sweep(i, 0, p, False), lo + 1, end - lo - 2, 3)
@@ -293,24 +283,38 @@
             span(lambda p: cond(i, 2, p), lo + 2, end - 1 - lo, 4)
             waits(i)
             span(lambda p: sweep(i, 2, p, False), lo + 3, end - 3 - lo, 5 if i == 0 else 2)
-            if i == 0:
-                near_copy(U1, near_send.at[1], near_recv.at[1]).start()
+
+        early(0)
+
+        def both():
+            near_copy(U1, near_send.at[1], near_recv.at[1]).start()
+            early(1)
+        if second is True:
+            both()
+        else:
+            pl.when(second)(both)
+        hook()
 
         def wave(j, c):
             @pl.when(has_far)
             def _():
-                for k in range(2):
-                    copy = far_copy(U0, far_send, far_recv, 2 * j + k)
-                    copy.wait_send()
-                    copy.wait_recv()
-            p = first - 1 - 2 * j
-            for i in range(2):
+                copy = far_copy(U0, far_send, far_recv, j)
+                copy.wait_send()
+                copy.wait_recv()
+
+            def part(i):
+                p = first - 1 - 2 * j + SWEEPS * i
                 for k in range(SWEEPS):
                     cond(i, k, p)
                     cond(i, k, p - 1)
                     p = p + 1
                     sweep(i, k, p, True)
                     sweep(i, k, p - 1, True)
+            part(0)
+            if second is True:
+                part(1)
+            else:
+                pl.when(second)(lambda: part(1))
             return c
         lax.fori_loop(0, FAR // 2, wave, 0)
 
@@ -331,18 +335,20 @@
 
     near_wait(KP.at[0], cf_s.at[0, FAR], cf_r.at[0, FAR])
     near_wait(HS.at[0], cf_s.at[1, FAR], cf_r.at[1, FAR])
-    far_wait(KP.at[0], cf_s.at[0], cf_r.at[0], range(FAR))
-    far_wait(HS.at[0], cf_s.at[1], cf_r.at[1], range(FAR))
-
-    def scale(z, c):
-        KP[1, z] = STEPS_DEV * KP[0, z]
-        HS[1, z] = STEPS_DEV * HS[0, z]
-        return c
-    lax.fori_loop(0, top, scale, 0)
-
-    def v_pair(n, coefs, terms, waits):
+
+    def coefficients():
+        far_wait(KP.at[0], cf_s.at[0], cf_r.at[0], range(FAR // 2))
+        far_wait(HS.at[0], cf_s.at[1], cf_r.at[1], range(FAR // 2))
+
+        def scale(z, c):
+            KP[1, z] = STEPS_DEV * KP[0, z]
+            HS[1, z] = STEPS_DEV * HS[0, z]
+            return c
+        lax.fori_loop(0, top, scale, 0)
+
+    def v_pair(n, coefs, terms, waits, hook):
         par = lax.rem(lax.div(n, 2), 2)
-        pair(v_state, n, coefs, terms, waits, (vf_s.at[par], vf_r.at[par]), (vn_s, vn_r))
+        pair(v_state, n, coefs, terms, waits, (vf_s.at[par], vf_r.at[par]), (vn_s, vn_r), hook, True)
 
     def v_send(n):
         par = lax.rem(lax.div(n, 2), 2)
@@ -357,7 +363,7 @@
         @pl.when(m > 0)
         def _():
             v_send(n)
-        v_pair(n, (0, 0), (None, None), no_wait)
+        v_pair(n, (0, 0), (None, None), no_wait, lambda: pl.when(m == 0)(coefficients))
 
         @pl.when(m == STEPS_DEV // 2)
         def _():
@@ -379,12 +385,21 @@
         return remote(V.at[n, inner], REL, rel_s.at[k], rel_r, tt, s)
 
     def ct_copy(i, h):
-        return remote(CT, CTB.at[i, pl.ds(own_lo - NEAR, depth)], ct_s.at[h, 0], ct_r.at[i, 0], n_slab + h, s)
-
-    def ct_far_copy(i, h):
-        mine = odd * (depth - NEAR)
+        return remote(CT, CTB.at[i, pl.ds(own_lo - NEAR, depth)], ct_s.at[h], ct_r.at[i], n_slab + h, s)
+
+    def halo_copy(i):
+        par = lax.rem(i, 2)
         there = (1 - odd) * depth
-        return remote(CT.at[pl.ds(mine, NEAR)], CTB.at[i, pl.ds(there, NEAR)], ct_s.at[h, 1], ct_r.at[i, 1], n_slab + h, far_s)
+        return remote(
+            CTB.at[2 * i, pl.ds(lowest(FAR, NEAR) - NEAR, NEAR)], CTB.at[2 * i, pl.ds(there, NEAR)],
+            th_s.at[par], th_r.at[par], t, far_s)
+
+    def halo_start(i):
+        ct_copy(2 * i, 0).wait_recv()
+
+        @pl.when(has_far)
+        def _():
+            halo_copy(i).start()
 
     def bef_copy(n, i):
         return remote(V.at[n, inner], F.at[0, inner], bef_s.at[i, 0], bef_r, i, s)
@@ -408,7 +423,9 @@
     def f_pair(n, par):
         near_copy(F.at[n], fn_s.at[0], fn_r.at[0]).start()
         far_start(F.at[n], ff_s.at[par], ff_r.at[par])
-        pair(f_state, n, (0, 0), (None, None), no_wait, (ff_s.at[par], ff_r.at[par]), (fn_s, fn_r))
+        pair(
+            f_state, n, (0, 0), (None, None), no_wait, (ff_s.at[par], ff_r.at[par]), (fn_s, fn_r), lambda: None,
+            par == 0)
 
     def f_both(c):
         def one(m, c):
@@ -439,15 +456,29 @@
         def advance(i, c):
             n = 2 * STEPS_DEV + 2 * i
             v_send(n)
-            hand_out(2 * i + 1, n)
+            @pl.when(2 * i + 1 < n_slab - 1)
+            def _():
+                hand_out(2 * i + 1, n)
+
+            @pl.when(i == 0)
+            def _():
+                halo_start(i)
 
             def waits(k):
-                ct_copy(2 * i + k, 0).wait_recv()
-                if k == 0:
-                    @pl.when(has_far)
-                    def _():
-                        ct_far_copy(2 * i, 0).wait_recv()
-            v_pair(n, (1, 1), (CTB.at[2 * i], CTB.at[2 * i + 1]), waits)
+                if k == 1:
+                    ct_copy(2 * i + 1, 0).wait_recv()
+
+            def hook():
+                @pl.when(has_far)
+                def _():
+                    copy = halo_copy(i)
+                    copy.wait_send()
+                    copy.wait_recv()
+            v_pair(n, (1, 1), (CTB.at[2 * i], CTB.at[2 * i + 1]), waits, hook)
+
+            @pl.when(2 * i + 2 < n_slab)
+            def _():
+                halo_start(i + 1)
             hand_out(2 * i + 2, n + 1)
             for k in range(2):
                 @pl.when(2 * i + k + WINDOW < n_slab)
@@ -456,6 +487,7 @@
                         credit.at[zh], inc=1, device_id=(2 * i + k + WINDOW, s), device_id_type=MESH)
             return c
         lax.fori_loop(0, n_slab // 2, advance, 0)
+        hand_out(n_slab - 1, begin + n_slab - 1)
 
         def last(z):
             OWN[z] = V[begin + n_slab + zh, own_lo + z]
@@ -472,14 +504,17 @@
                 pl.semaphore_wait(credit.at[h], 1)
             ct_copy(t, h).start()
 
-            @pl.when((zh == 0) & has_far)
-            def _():
-                ct_far_copy(t, h).start()
+        @pl.when(t >= n_slab - STEPS_DEV)
+        def _():
+            rel_copy(STEPS_DEV, t_next, 0).start()
 
         @pl.when(t > 0)
         def _():
             bef_copy(0, t).wait_recv()
-        rel_copy(STEPS_DEV, t_next, 0).start()
+
+        @pl.when(t < n_slab - STEPS_DEV)
+        def _():
+            rel_copy(STEPS_DEV, t_next, 0).start()
 
     @pl.when(is_home)
     def _():
@@ -501,10 +536,6 @@
         rel_copy(STEPS_DEV, t_next, 0).wait_send()
         for h in range(2):
             ct_copy(t, h).wait_send()
-
-            @pl.when((zh == 0) & has_far)
-            def _():
-                ct_far_copy(t, h).wait_send()
 
     @pl.when(t == n_slab)
     def _():
@@ -560,7 +591,7 @@
                 dma((2, FAR + 1)), dma((2, FAR + 1)),
                 dma((2, FAR)), dma((2, FAR)), dma((2,)), dma((2,)),
                 dma((2, FAR)), dma((2, FAR)), dma((2,)), dma((2,)),
-                dma((2,)), dma, dma((n_tm, 2)), dma, dma, dma((2, 2)), dma((n_tm, 2)),
+                dma((2,)), dma, dma((n_tm, 2)), dma, dma, dma((2,)), dma((n_tm,)), dma((2,)), dma((2,)),
                 pltpu.SemaphoreType.REGULAR((2,)),
             ],
             compiler_params=pltpu.CompilerParams(

time: 227 us -> 213 us (0.938)
  the two profiles are of different devices: /device:TPU:151 before, /device:TPU:29 now
where the time goes in v3:
time: 213 us
  Pallas kernels  209 us (98%)
  local copies, waits for them, and re-layouts  3.06 us (1%)
    pallas_call x1, Pallas kernels, per_device(): pl.pallas_call(functools.partial(kernel, n_tm, n_sp), out_shape=(jax.Shap...  209 us

profile of v3, /device:TPU:29, one launch (start us, length us, event | category | flops | bytes accessed | tf_op | source)
XLA Modules:
  0.0 213.2 jit_solution(7919709799791223108)
XLA Ops:
  0.6 209.4 %shard_map.59 = (f32[4,8,32,256]{3,2,1,0:T(8,128)}, f32[1,8,32,256]{3,2,1,0:T(8,128)}) custom-call(f32[1,8,32,256]{3,2,1,0:T(8,128)} %cg.1, f32[8,32,256]{2,1,0:T(8,128)} %u0.1, f32[8,32,256]{2,1,0:T(8,128)} %kap.1, f32[8,32,256]{2,1,0:T(8,128)} %src.1), custom_call_target="tpu_custom_call" | custom-call | tf_op jit(solution)/shard_map/pallas_call | solution.py:570
  210.1 0.0 copy-start
  210.1 2.4 %copy.8 = f32[4,8,32,256]{3,2,1,0:T(8,128)} copy(f32[4,8,32,256]{3,2,1,0:T(8,128)} %get-tuple-element.4) | data formatting | bytes 2097152
  212.4 0.0 copy-done
  212.5 0.7 copy.9
Async XLA Ops:
  210.1 2.4 %copy-start = (f32[1,8,32,256]{3,2,1,0:T(8,128)S(1)}, f32[1,8,32,256]{3,2,1,0:T(8,128)}, u32[]{:S(2)}) copy-start(f32[1,8,32,256]{3,2,1,0:T(8,128)} %get-tuple-element.5) | copy-start | bytes 786436

commit v4 on v3

--- a/solution.py
+++ b/solution.py
@@ -19,9 +19,9 @@
 
 def kernel(
     n_tm, n_sp, cg, u0, kap, src, fine, pc,
-    V, F, KP, HS, T, K, G, NAT, CT, CTB, REL, OWN,
+    V, F, KP, HS, T, K, G, NAT, CT, CTB, REL, OWN, RB,
     cf_s, cf_r, vf_s, vf_r, vn_s, vn_r, ff_s, ff_r, fn_s, fn_r,
-    rel_s, rel_r, bef_s, bef_r, own_r, ct_s, ct_r, th_s, th_r, credit,
+    rel_s, rel_r, bef_s, bef_r, own_r, ct_s, ct_r, th_s, th_r, rb_r, rl_s, credit,
 ):
     depth, nx, ny = u0.shape
     xf_n = nx // 8
@@ -29,6 +29,7 @@
     top = FAR + depth + NEAR
     t, s = lax.axis_index("tm"), lax.axis_index("space")
     n_slab = n_tm - 2
+    lane_t = n_tm // 4
     zh = lax.rem(t, 2)
     is_home = t >= n_slab
     not_home = t < n_slab
@@ -58,6 +59,15 @@
         pl.semaphore_signal(barrier, inc=1, device_id=(tt, ss), device_id_type=MESH)
 
     greet(t, near_s)
+    relays, relayed = t < lane_t, (t >= lane_t) & (t < 2 * lane_t)
+
+    @pl.when(relays)
+    def _():
+        greet(t + lane_t, s)
+
+    @pl.when(relayed)
+    def _():
+        greet(t - lane_t, s)
     greet(t_next, s)
     greet(t_prev, s)
 
@@ -139,7 +149,7 @@
         for i in (0, 2):
             F[i, layers(0, FAR)] = zero
 
-    greeted = 3 + far_i + jnp.where(is_home, n_slab, 2)
+    greeted = 3 + far_i + jnp.where(is_home, n_slab, 2) + jnp.where(t < 2 * lane_t, 1, 0)
     pl.semaphore_wait(barrier, greeted)
 
     def remote(src_ref, dst_ref, send, recv, tt, ss):
@@ -409,16 +419,27 @@
 
     begin = 2 * STEPS_DEV - 1
 
+    def relay_in(n, i, k):
+        return remote(V.at[n, inner], RB.at[k], bef_s.at[i, k], rb_r.at[k], i - lane_t, s)
+
+    def relay_out(k):
+        dst, recv = ((F.at[0, inner], bef_r), (OWN, own_r))[k]
+        return remote(RB.at[k], dst, rl_s.at[k], recv, t + lane_t, s)
+
     def hand_out(d, n):
+        d = jnp.asarray(d, jnp.int32)
         to_own = lax.rem(d + zh, 2) == 0
-
-        @pl.when(to_own & (d < n_slab))
-        def _():
-            own_copy(n, d).start()
-
-        @pl.when(jnp.logical_not(to_own) & (d + 1 < n_slab))
-        def _():
-            bef_copy(n, d + 1).start()
+        for k, e, wanted in ((0, d + 1, jnp.logical_not(to_own)), (1, d, to_own)):
+            wanted = wanted & (e < n_slab)
+            by_relay = (e >= lane_t) & (e < 2 * lane_t)
+
+            @pl.when(wanted & by_relay)
+            def _():
+                relay_in(n, e, k).start()
+
+            @pl.when(wanted & jnp.logical_not(by_relay))
+            def _():
+                (bef_copy, own_copy)[k](n, e).start()
 
     def f_pair(n, par):
         near_copy(F.at[n], fn_s.at[0], fn_r.at[0]).start()
@@ -464,9 +485,17 @@
             def _():
                 halo_start(i)
 
+            def release():
+                for k in range(2):
+                    @pl.when(2 * i + k + WINDOW < n_slab)
+                    def _():
+                        pl.semaphore_signal(
+                            credit.at[zh], inc=1, device_id=(2 * i + k + WINDOW, s), device_id_type=MESH)
+
             def waits(k):
                 if k == 1:
                     ct_copy(2 * i + 1, 0).wait_recv()
+                    release()
 
             def hook():
                 @pl.when(has_far)
@@ -480,11 +509,6 @@
             def _():
                 halo_start(i + 1)
             hand_out(2 * i + 2, n + 1)
-            for k in range(2):
-                @pl.when(2 * i + k + WINDOW < n_slab)
-                def _():
-                    pl.semaphore_signal(
-                        credit.at[zh], inc=1, device_id=(2 * i + k + WINDOW, s), device_id_type=MESH)
             return c
         lax.fori_loop(0, n_slab // 2, advance, 0)
         hand_out(n_slab - 1, begin + n_slab - 1)
@@ -530,6 +554,14 @@
     rel_copy(STEPS_DEV, t_next, 0).wait_recv()
     to_outside(lambda z: OWN[z], fine.at[STEPS_DEV - 1])
     to_outside(lambda z: OWN[z] - REL[z], pc.at[0])
+
+    @pl.when(relays)
+    def _():
+        for k in range(2):
+            relay_in(0, t + lane_t, k).wait_recv()
+            relay_out(k).start()
+        for k in range(2):
+            relay_out(k).wait_send()
 
     @pl.when(not_home)
     def _():
@@ -588,10 +620,11 @@
                 pltpu.VMEM((n_terms, depth + NEAR) + plane, f32),
                 pltpu.VMEM((depth,) + plane, f32),
                 pltpu.VMEM((depth,) + plane, f32),
+                pltpu.VMEM((2, depth) + plane, f32),
                 dma((2, FAR + 1)), dma((2, FAR + 1)),
                 dma((2, FAR)), dma((2, FAR)), dma((2,)), dma((2,)),
                 dma((2, FAR)), dma((2, FAR)), dma((2,)), dma((2,)),
-                dma((2,)), dma, dma((n_tm, 2)), dma, dma, dma((2,)), dma((n_tm,)), dma((2,)), dma((2,)),
+                dma((2,)), dma, dma((n_tm, 2)), dma, dma, dma((2,)), dma((n_tm,)), dma((2,)), dma((2,)), dma((2,)), dma((2,)),
                 pltpu.SemaphoreType.REGULAR((2,)),
             ],
             compiler_params=pltpu.CompilerParams(

time: 213 us -> 202 us (0.948)
  the two profiles are of different devices: /device:TPU:29 before, /device:TPU:151 now
where the time goes in v4:
time: 202 us
  Pallas kernels  198 us (98%)
  local copies, waits for them, and re-layouts  3.06 us (2%)
    pallas_call x1, Pallas kernels, per_device(): pl.pallas_call(functools.partial(kernel, n_tm, n_sp), out_shape=(jax.Shap...  198 us

profile of v4, /device:TPU:151, one launch (start us, length us, event | category | flops | bytes accessed | tf_op | source)
XLA Modules:
  0.0 201.7 jit_solution(6549590494044263497)
XLA Ops:
  0.6 198.0 %shard_map.59 = (f32[4,8,32,256]{3,2,1,0:T(8,128)}, f32[1,8,32,256]{3,2,1,0:T(8,128)}) custom-call(f32[1,8,32,256]{3,2,1,0:T(8,128)} %cg.1, f32[8,32,256]{2,1,0:T(8,128)} %u0.1, f32[8,32,256]{2,1,0:T(8,128)} %kap.1, f32[8,32,256]{2,1,0:T(8,128)} %src.1), custom_call_target="tpu_custom_call" | custom-call | tf_op jit(solution)/shard_map/pallas_call | solution.py:602
  198.6 0.0 copy-start
  198.6 2.4 %copy.8 = f32[4,8,32,256]{3,2,1,0:T(8,128)} copy(f32[4,8,32,256]{3,2,1,0:T(8,128)} %get-tuple-element.4) | data formatting | bytes 2097152
  201.0 0.0 copy-done
  201.0 0.7 copy.9
Async XLA Ops:
  198.6 2.4 %copy-start = (f32[1,8,32,256]{3,2,1,0:T(8,128)S(1)}, f32[1,8,32,256]{3,2,1,0:T(8,128)}, u32[]{:S(2)}) copy-start(f32[1,8,32,256]{3,2,1,0:T(8,128)} %get-tuple-element.5) | copy-start | bytes 786436

commit v5 on v4

--- a/solution.py
+++ b/solution.py
@@ -493,9 +493,10 @@
                             credit.at[zh], inc=1, device_id=(2 * i + k + WINDOW, s), device_id_type=MESH)
 
             def waits(k):
-                if k == 1:
+                if k == 0:
+                    release()
+                else:
                     ct_copy(2 * i + 1, 0).wait_recv()
-                    release()
 
             def hook():
                 @pl.when(has_far)

time: 202 us -> 197 us (0.975)
  Pallas kernels: 198 us -> 194 us
    pallas_call x1, Pallas kernels: 198 us -> 194 us  [per_device(): pl.pallas_call(functools.partial(kernel, n_tm, n_sp), out_shape=(jax.Shap...]
where the time goes in v5:
time: 197 us
  Pallas kernels  194 us (98%)
  local copies, waits for them, and re-layouts  3.06 us (2%)
    pallas_call x1, Pallas kernels, per_device(): pl.pallas_call(functools.partial(kernel, n_tm, n_sp), out_shape=(jax.Shap...  194 us

profile of v5, /device:TPU:151, one launch (start us, length us, event | category | flops | bytes accessed | tf_op | source)
XLA Modules:
  0.0 197.3 jit_solution(17615764019320676303)
XLA Ops:
  0.6 193.6 %shard_map.59 = (f32[4,8,32,256]{3,2,1,0:T(8,128)}, f32[1,8,32,256]{3,2,1,0:T(8,128)}) custom-call(f32[1,8,32,256]{3,2,1,0:T(8,128)} %cg.1, f32[8,32,256]{2,1,0:T(8,128)} %u0.1, f32[8,32,256]{2,1,0:T(8,128)} %kap.1, f32[8,32,256]{2,1,0:T(8,128)} %src.1), custom_call_target="tpu_custom_call" | custom-call | tf_op jit(solution)/shard_map/pallas_call | solution.py:603
  194.2 0.0 copy-start
  194.2 2.4 %copy.8 = f32[4,8,32,256]{3,2,1,0:T(8,128)} copy(f32[4,8,32,256]{3,2,1,0:T(8,128)} %get-tuple-element.4) | data formatting | bytes 2097152
  196.6 0.0 copy-done
  196.6 0.7 copy.9
Async XLA Ops:
  194.2 2.4 %copy-start = (f32[1,8,32,256]{3,2,1,0:T(8,128)S(1)}, f32[1,8,32,256]{3,2,1,0:T(8,128)}, u32[]{:S(2)}) copy-start(f32[1,8,32,256]{3,2,1,0:T(8,128)} %get-tuple-element.5) | copy-start | bytes 786436
